TPU v7x, 256 devices: a whole 4x4x8 slice. The times are simulated.
256 devices in a mesh: pb: 8 (over z_hi, core), ka: 32 (over y, x, z_lo).
Axes of the slice: x: 4, y: 4, z: 8 (z_hi: 4, z_lo: 2; z = z_hi * 2 + z_lo), core: 2. Of those that a mesh axis runs over, the one named last changes fastest.
Arguments:
- queries: bfloat16 [40960, 128], P(('pb', 'ka')), may hold values from -6 to 6
- keys_in: bfloat16 [40960, 128], P(('pb', 'ka')), may hold values from -6 to 6
- values_in: bfloat16 [40960, 128], P(('pb', 'ka')), may hold values from -6 to 6
- outputs_saved: bfloat16 [40960, 128], P(('pb', 'ka')), may hold values from -6 to 6
- out_grad: bfloat16 [40960, 128], P(('pb', 'ka')), may hold values from -24 to 24
- log_sum: float32 [40960], P(('pb', 'ka'))
- block_table: int32 [512], replicated, may hold values from 0 to 511, as said below
Outputs:
- grad_queries: bfloat16 [40960, 128], P(('pb', 'ka'))
- grad_keys: bfloat16 [40960, 128], P(('pb', 'ka'))
- grad_values: bfloat16 [40960, 128], P(('pb', 'ka'))
Inputs may be any that keep to these rules, and one draw needn't show every extreme that they name: block_table is a permutation: storage block b holds the segment's tokens 80 * block_table[b] to 80 * block_table[b] + 79.
All inputs are finite; a program needn't handle non-finite values.
Results may differ from a plain program's by a relative error of at most 0.0069.
Values may be sent and summed in bfloat16 or wider, within the bound.
A program may use at most 64 MiB of HBM per device.

v0:
```python
import math

import jax
import jax.numpy as jnp
from jax import lax
from jax.sharding import PartitionSpec as P


def per_device(queries, keys_in, values_in, outputs_saved, out_grad, log_sum, block_table):
    tok_rows = queries.shape[0]
    width = queries.shape[1]
    blk_rows = tok_rows // 2
    scale = 1.0 / width**0.5
    n_key = lax.axis_size("ka")
    n_query = lax.axis_size("pb")
    table3 = block_table.reshape(n_query, n_key, 2)
    q_table = lax.dynamic_index_in_dim(table3, lax.axis_index("pb"), 0, keepdims=False).reshape(-1)
    k_table = lax.dynamic_index_in_dim(table3, lax.axis_index("ka"), 1, keepdims=False).reshape(-1)
    offsets = jnp.arange(blk_rows, dtype=jnp.int32)
    q_position = (q_table[:, None] * blk_rows + offsets[None, :]).reshape(-1)
    k_position = (k_table[:, None] * blk_rows + offsets[None, :]).reshape(-1)
    q_all, o_all, g_all = (
        lax.all_gather(queries, "ka", axis=0, tiled=True),
        lax.all_gather(outputs_saved, "ka", axis=0, tiled=True),
        lax.all_gather(out_grad, "ka", axis=0, tiled=True),
    )
    l_all = lax.all_gather(log_sum, "ka", axis=0, tiled=True)
    d_all = jnp.sum(g_all.astype(jnp.float32) * o_all.astype(jnp.float32), axis=1)
    k_all, v_all = (
        lax.all_gather(keys_in, "pb", axis=0, tiled=True),
        lax.all_gather(values_in, "pb", axis=0, tiled=True),
    )

    def tile_terms(q_b, g_b, l_b, d_b, pos_b):
        scores = (
            lax.dot_general(
                q_b, k_all, (((1,), (1,)), ((), ())), preferred_element_type=jnp.float32
            )
            * scale
        )
        visible = pos_b[:, None] >= k_position[None, :]
        probs = jnp.where(visible, jnp.exp(scores - l_b[:, None]), 0.0)
        dprobs = lax.dot_general(
            g_b, v_all, (((1,), (1,)), ((), ())), preferred_element_type=jnp.float32
        )
        dscores = (probs * (dprobs - d_b[:, None]) * scale).astype(jnp.bfloat16)
        return (probs, dscores)

    group = math.gcd(n_key, 4)
    rows_blk = tok_rows * group
    count = n_key // group
    q_blocks = q_all.reshape(count, rows_blk, width)
    g_blocks = g_all.reshape(count, rows_blk, width)
    l_blocks = l_all.reshape(count, rows_blk)
    d_blocks = d_all.reshape(count, rows_blk)
    p_blocks = q_position.reshape(count, rows_blk)
    zeros = jnp.zeros((k_all.shape[0], width), jnp.float32)

    def step(carry, item):
        grad_k, grad_v = carry
        q_b, g_b, l_b, d_b, pos_b = item
        probs, dscores = tile_terms(q_b, g_b, l_b, d_b, pos_b)
        probs_b = probs.astype(jnp.bfloat16)
        grad_v = grad_v + lax.dot_general(
            probs_b, g_b, (((0,), (0,)), ((), ())), preferred_element_type=jnp.float32
        )
        grad_k = grad_k + lax.dot_general(
            dscores, q_b, (((0,), (0,)), ((), ())), preferred_element_type=jnp.float32
        )
        grad_q = jnp.dot(dscores, k_all, preferred_element_type=jnp.float32)
        return ((grad_k, grad_v), grad_q)

    (grad_k, grad_v), grad_q = lax.scan(
        step, (zeros, zeros), (q_blocks, g_blocks, l_blocks, d_blocks, p_blocks)
    )
    grad_q = grad_q.reshape(q_all.shape[0], width)
    own_q = lax.psum_scatter(grad_q, "ka", scatter_dimension=0, tiled=True)
    own_k, own_v = (
        lax.psum_scatter(grad_k, "pb", scatter_dimension=0, tiled=True),
        lax.psum_scatter(grad_v, "pb", scatter_dimension=0, tiled=True),
    )
    return (own_q.astype(jnp.bfloat16), own_k.astype(jnp.bfloat16), own_v.astype(jnp.bfloat16))


def solution(mesh):
    return jax.shard_map(
        per_device,
        mesh=mesh,
        in_specs=(
            P(("pb", "ka"), None),
            P(("pb", "ka"), None),
            P(("pb", "ka"), None),
            P(("pb", "ka"), None),
            P(("pb", "ka"), None),
            P(("pb", "ka")),
            P(),
        ),
        out_specs=(P(("pb", "ka"), None), P(("pb", "ka"), None), P(("pb", "ka"), None)),
        check_vma=False,
    )
```

profile of v0, /device:TPU:2, one launch (start us, length us, event | category | flops | bytes accessed | tf_op | source)
XLA Modules:
  0.0 799.1 jit_solution(8593101088611219314)
XLA Ops:
  12.4 155.3 %all-reduce = f32[5120]{0:T(1024)S(1)} all-reduce(f32[5120]{0:T(1024)S(1)} %dynamic-update-slice), channel_id=1, replica_groups=mesh['pb'=8,'ka'=32] {'ka'}, use_global_device_ids=true, to_apply=%add | all-reduce | flops 5120 | bytes 40960
  168.9 18.0 %all_gather.19 = bf16[1280,128]{1,0:T(8,128)(2,1)S(1)} all-gather(bf16[160,128]{1,0:T(8,128)(2,1)} %param.10), channel_id=1, replica_groups=mesh['pb'=8,'ka'=32] {'pb'}, dimensions={0}, use_global_device_ids=true | all-gather | bytes 368640 | tf_op jit(solution)/shard_map/all_gather | solution.py:30
  186.9 15.0 %all_gather.22 = bf16[1280,128]{1,0:T(8,128)(2,1)S(1)} all-gather(bf16[160,128]{1,0:T(8,128)(2,1)} %param.11), channel_id=1, replica_groups=mesh['pb'=8,'ka'=32] {'pb'}, dimensions={0}, use_global_device_ids=true | all-gather | bytes 368640 | tf_op jit(solution)/shard_map/all_gather | solution.py:31
  202.0 118.0 %all-gather.6.cloned.1.call-done = bf16[5120,128]{1,0:T(8,128)(2,1)} async-done(((bf16[160,128]{1,0:T(8,128)(2,1)}), bf16[5120,128]{1,0:T(8,128)(2,1)}) %all-gather.6.cloned.1.call-update) | async-done | bytes 1310736 | tf_op jit(solution)/shard_map/all_gather | solution.py:25
  319.9 2.5 multiply_reduce_fusion
  322.4 154.3 %all-gather.4.cloned.1.call-done = bf16[5120,128]{1,0:T(8,128)(2,1)} async-done(((bf16[160,128]{1,0:T(8,128)(2,1)}), bf16[5120,128]{1,0:T(8,128)(2,1)}) %all-gather.4.cloned.1.call-update) | async-done | bytes 1310736 | tf_op jit(solution)/shard_map/all_gather | solution.py:23
  476.8 66.7 %while.15 = (s32[]{:T(128)}, f32[1280,128]{1,0:T(8,128)S(1)}, f32[1280,128]{1,0:T(8,128)S(1)}, f32[8,640,128]{2,1,0:T(8,128)}, s32[8,640]{1,0:T(8,128)S(1)}, /*i...) while((s32[]{:T(128)}, f32[1280,128]{1,0:T(8,128)S(1)}, ...), condition=%wide.region_2.3_spmd.clone, body=%wide.region_1.2_spmd.clone.sunk | while | flops 1056605440 | bytes 19376884 | solution.py:73
  477.0 1.8 fusion.50
  478.7 1.7 convolution_add_fusion.5
  485.3 1.8 fusion.50
  487.1 1.7 convolution_add_fusion.5
  493.6 1.8 fusion.50
  495.4 1.7 convolution_add_fusion.5
  502.0 1.8 fusion.50
  510.3 1.8 fusion.50
  512.1 1.7 convolution_add_fusion.5
  518.7 1.8 fusion.50
  520.5 1.7 convolution_add_fusion.5
  527.0 1.8 fusion.50
  528.8 1.7 convolution_add_fusion.5
  535.4 1.8 fusion.50
  545.5 41.5 %reduce-scatter.6.cloned.1.call-done = f32[160,128]{1,0:T(8,128)} async-done(((f32[1280,128]{1,0:T(8,128)}), f32[160,128]{1,0:T(8,128)}) %reduce-scatter.6.cloned.1.call-update) | async-done | bytes 81936 | tf_op jit(solution)/shard_map/reduce_scatter | solution.py:79
  588.5 36.8 %reduce-scatter.8.cloned.1.call-done = f32[160,128]{1,0:T(8,128)} async-done(((f32[1280,128]{1,0:T(8,128)}), f32[160,128]{1,0:T(8,128)}) %reduce-scatter.8.cloned.1.call-update) | async-done | bytes 81936 | tf_op jit(solution)/shard_map/reduce_scatter | solution.py:80
  626.8 163.9 %reduce-scatter.4.cloned.1.call-done = f32[160,128]{1,0:T(8,128)} async-done(((f32[5120,128]{1,0:T(8,128)}), f32[160,128]{1,0:T(8,128)}) %reduce-scatter.4.cloned.1.call-update) | async-done | bytes 81936 | tf_op jit(solution)/shard_map/reduce_scatter | solution.py:77
  (96 shorter events, 53.9 us)
Async XLA Ops:
  7.2 194.8 %all-gather.8.cloned.1.call-start = ((), (), s32[]{:S(2)}) async-start(), calls=%async_computation.5 | async-start | bytes 1351680 | tf_op jit(solution)/shard_map/all_gather | solution.py:24
  7.9 312.0 %all-gather.6.cloned.1.call-start = ((), (), s32[]{:S(2)}) async-start(), calls=%async_computation.4 | async-start | bytes 1351680 | tf_op jit(solution)/shard_map/all_gather | solution.py:25
  8.6 468.1 %all-gather.4.cloned.1.call-start = ((), (), s32[]{:S(2)}) async-start(), calls=%async_computation.3 | async-start | bytes 1351680 | tf_op jit(solution)/shard_map/all_gather | solution.py:23
  9.4 577.6 %reduce-scatter.6.cloned.1.call-start = ((), (), s32[]{:S(2)}) async-start(), calls=%async_computation.7 | async-start | bytes 737280 | tf_op jit(solution)/shard_map/reduce_scatter | solution.py:79
  543.5 0.8 copy-start
  543.5 1.1 copy-start.1
  544.4 80.9 %reduce-scatter.8.cloned.1.call-start = ((), (), s32[]{:S(2)}) async-start(), calls=%async_computation.8 | async-start | bytes 737280 | tf_op jit(solution)/shard_map/reduce_scatter | solution.py:80
  544.9 245.8 %reduce-scatter.4.cloned.1.call-start = ((), (), s32[]{:S(2)}) async-start(), calls=%async_computation.6 | async-start | bytes 2703360 | tf_op jit(solution)/shard_map/reduce_scatter | solution.py:77
Sparse Core Ops, SparseCore 0:
  9.8 153.7 all-gather.7
  165.4 154.5 all-gather.5
  321.7 154.9 all-gather.3
  544.5 42.4 reduce-scatter.5
  589.4 35.8 reduce-scatter.7
  627.6 163.0 reduce-scatter.3
where the time goes:
time: 804 us; the launch traced here: 799 us
  waiting for transfers between devices  517 us (64%)
  blocking collectives  188 us (23%)
  matrix products  64.9 us (8%)
  between operations  14.9 us (2%)
    reduce_scatter x1, waiting for transfers between devices, per_device(): own_q = lax.psum_scatter(grad_q, 'ka', scatter_dimension=0, tiled=True)  164 us
    unnamed x1, blocking collectives  155 us
    all_gather x1, waiting for transfers between devices, per_device(): lax.all_gather(queries, 'ka', axis=0, tiled=True)  154 us
    all_gather x1, waiting for transfers between devices, per_device(): lax.all_gather(out_grad, 'ka', axis=0, tiled=True)  118 us
    reduce_scatter x1, waiting for transfers between devices, per_device(): lax.psum_scatter(grad_k, 'pb', scatter_dimension=0, tiled=True)  41.5 us
    reduce_scatter x1, waiting for transfers between devices, per_device(): lax.psum_scatter(grad_v, 'pb', scatter_dimension=0, tiled=True)  36.8 us
    all_gather x1, blocking collectives, per_device(): lax.all_gather(keys_in, 'pb', axis=0, tiled=True)  18 us
  transfers between devices with their start and end apart: 6, of which 5 were waited for; matrix products, arithmetic and copies ran while one was open for 1% of the time, Pallas kernels for 0%

commit v1 on v0

v1 whole, which is shorter than its diff:
```python
import math

import jax
import jax.numpy as jnp
from jax import lax
from jax.experimental import pallas as pl
from jax.experimental.pallas import tpu as pltpu
from jax.sharding import PartitionSpec as P

MESH = pl.DeviceIdType.MESH
F32, BF16 = jnp.float32, jnp.bfloat16
ROWS = 160
BLK = 80
WIDTH = 128
SCALE = 1.0 / math.sqrt(WIDTH)
TO_EXP2 = SCALE * math.log2(math.e)
LOG2E = math.log2(math.e)
HIDDEN = 1e30
CHUNK = 336
PLANE = (
    (0, 0), (1, 0), (3, 0), (0, 1), (0, 3), (1, 1), (3, 3), (1, 3),
    (3, 1), (2, 0), (0, 2), (2, 1), (2, 3), (1, 2), (3, 2), (2, 2),
)
LINE = (0, 1, 7, 2, 6, 3, 5, 4)
Q_TILE, K_TILE = 8 * ROWS, 4 * ROWS
NT = (((1,), (1,)), ((), ()))
TN = (((0,), (0,)), ((), ()))


def plane_slot(dx, dy):
    return PLANE.index((dx % 4, dy % 4))


def line_slot(dz):
    return LINE.index(dz % 8)


def place():
    pb, ka = lax.axis_index("pb"), lax.axis_index("ka")
    x, y, z, c = (ka // 2) % 4, ka // 8, (pb // 2) * 2 + ka % 2, pb % 2
    return x, y, z, c


def device(x, y, z, c):
    return ((z // 2) * 2 + c, y * 8 + x * 2 + z % 2)


def storage(x, y, z, c):
    pb, ka = device(x, y, z, c)
    return pb * 32 + ka


def kernel(
    q_in, k_in, v_in, o_in, g_in, l_in, table,
    dq_out, dk_out, dv_out,
    qg, kv, o_own, dq_acc, dk_acc, dv_acc, lrow, drow, keyid,
    dq_send, dq_recv, sib_send, sib_recv, dkv_send, dkv_recv, dkv_cross,
    local_sem, q_ss, q_rs, kz_ss, kz_rs, kc_ss, kc_rs,
    dq_ss, dq_rs, sib_ss, sib_rs, dkv_ss, dkv_rs, cross_ss, cross_rs,
):
    x, y, z, c = place()
    other = 1 - c

    def plane_dev(i):
        dx, dy = PLANE[i]
        return device((x + dx) % 4, (y + dy) % 4, z, c)

    def line_dev(i):
        return device(x, y, (z + LINE[i]) % 8, c)

    sibling = device(x, y, z, other)
    cross_up = device(x, y, (z + 1) % 8, other)
    cross_down = device(x, y, (z + 7) % 8, other)
    partners = [plane_dev(i) for i in range(1, 16)]
    partners += [line_dev(i) for i in range(1, 8)]
    partners += [sibling, cross_up, cross_down]
    barrier = pltpu.get_barrier_semaphore()
    for p in partners:
        pl.semaphore_signal(barrier, inc=1, device_id=p, device_id_type=MESH)

    loads = [
        pltpu.make_async_copy(g_in, qg.at[0, pl.ds(ROWS, ROWS)], local_sem.at[0]),
        pltpu.make_async_copy(o_in, o_own, local_sem.at[1]),
        pltpu.make_async_copy(q_in, qg.at[0, pl.ds(0, ROWS)], local_sem.at[2]),
        pltpu.make_async_copy(k_in, kv.at[0, 0, 0], local_sem.at[3]),
        pltpu.make_async_copy(v_in, kv.at[1, 0, 0], local_sem.at[4]),
    ]
    for cp in loads:
        cp.start()
    dq_acc[...] = jnp.zeros_like(dq_acc)
    dk_acc[...] = jnp.zeros_like(dk_acc)
    dv_acc[...] = jnp.zeros_like(dv_acc)
    for cp in loads:
        cp.wait()

    q0, g0 = qg[0, 0:ROWS, :], qg[0, ROWS : 2 * ROWS, :]
    k0, v0 = kv[0, 0, 0], kv[1, 0, 0]
    prod = g0.astype(F32) * o_own[...].astype(F32)
    high = prod.astype(BF16)
    low = (prod - high.astype(F32)).astype(BF16)
    ones = jnp.ones((8, WIDTH), BF16)
    delta8 = lax.dot_general(ones, high, NT, preferred_element_type=F32)
    delta8 += lax.dot_general(ones, low, NT, preferred_element_type=F32)
    delta = delta8[0:1, :]
    lse = l_in[...] * LOG2E
    sub = lax.broadcasted_iota(jnp.int32, (8, ROWS), 0)
    both = jnp.where(sub % 2 == 0, lse, delta)
    p1 = both.astype(BF16).astype(F32)
    p2 = (both - p1).astype(BF16).astype(F32)
    p3 = both - p1 - p2
    pieces = jnp.where(sub < 2, p1, jnp.where(sub < 4, p2, jnp.where(sub < 6, p3, 0.0)))
    wide = jnp.concatenate([pieces, jnp.zeros((8, 256 - ROWS), F32)], axis=1)
    first, rest = wide[:, 0:128], wide[:, 128:256]
    lane = lax.broadcasted_iota(jnp.int32, (8, 128), 1)
    second = jnp.where(
        lane < 48, pltpu.roll(first, 48, 1), pltpu.roll(rest, 48, 1)
    )
    keep = lane < BLK
    stats = jnp.concatenate(
        [jnp.where(keep, first, 0.0), jnp.where(keep, second, 0.0)], axis=0
    )
    qg[0, 2 * ROWS : CHUNK, :] = stats.astype(BF16)

    pl.semaphore_wait(barrier, len(partners))

    q_cps, kz_cps = {}, {}
    for i in range(1, 16):
        dx, dy = PLANE[i]
        q_cps[i] = pltpu.make_async_remote_copy(
            src_ref=qg.at[0], dst_ref=qg.at[plane_slot(-dx, -dy)],
            send_sem=q_ss.at[i], recv_sem=q_rs.at[plane_slot(-dx, -dy)],
            device_id=plane_dev(i), device_id_type=MESH,
        )
    for i in range(1, 8):
        to = line_slot(-LINE[i])
        kz_cps[i] = pltpu.make_async_remote_copy(
            src_ref=kv.at[:, 0, 0], dst_ref=kv.at[:, to, 0],
            send_sem=kz_ss.at[i], recv_sem=kz_rs.at[to],
            device_id=line_dev(i), device_id_type=MESH,
        )
    kc_cps = [
        pltpu.make_async_remote_copy(
            src_ref=kv.at[:, s, 0], dst_ref=kv.at[:, s, 1],
            send_sem=kc_ss.at[s], recv_sem=kc_rs.at[s],
            device_id=sibling, device_id_type=MESH,
        )
        for s in range(8)
    ]
    kc_cps[0].start()
    for i in (1, 2):
        kz_cps[i].start()
    for i in range(1, 5):
        q_cps[i].start()
    for i in (3, 4):
        kz_cps[i].start()
    for i in range(5, 9):
        q_cps[i].start()
    for i in (5, 6, 7):
        kz_cps[i].start()
    for i in range(9, 16):
        q_cps[i].start()

    def q_arrived(i):
        dx, dy = PLANE[i]
        q_cps[plane_slot(-dx, -dy)].wait_recv()

    def kz_arrived(s):
        kz_cps[line_slot(-LINE[s])].wait_recv()

    row = lax.broadcasted_iota(jnp.int32, (ROWS, ROWS), 0)
    col = lax.broadcasted_iota(jnp.int32, (ROWS, ROWS), 1)
    seen = (row <= col) & ((row >= BLK) == (col >= BLK))
    s0 = lax.dot_general(k0, q0, NT, preferred_element_type=F32)
    e0 = jnp.exp2(jnp.where(seen, s0 * TO_EXP2 - lse, -HIDDEN))
    dp0 = lax.dot_general(v0, g0, NT, preferred_element_type=F32)
    ds0 = (e0 * (dp0 - delta)).astype(BF16)
    dq_acc[0:ROWS, :] = lax.dot_general(ds0, k0, TN, preferred_element_type=F32)
    dk_acc[0:ROWS, :] = jnp.dot(ds0, q0, preferred_element_type=F32)
    dv_acc[0:ROWS, :] = jnp.dot(e0.astype(BF16), g0, preferred_element_type=F32)

    for r in range(32):
        s, h, b = r // 4, (r % 4) // 2, r % 2
        at = storage(x, y, (z + LINE[s]) % 8, c if h == 0 else other) * 2 + b
        keyid[r : r + 1, :] = jnp.full((1, 128), table[at], jnp.int32)

    def rows_of(half):
        blocks = []
        for i in range(8 * half, 8 * half + 8):
            st = qg[i, 2 * ROWS : CHUNK, :].astype(F32)
            dx, dy = PLANE[i]
            at = storage((x + dx) % 4, (y + dy) % 4, z, c) * 2
            blocks += [(st[0:8, :], table[at]), (st[8:16, :], table[at + 1])]
        for j in range(10):
            acc = jnp.zeros((8, 128), F32)
            ids = jnp.zeros((8, 128), jnp.int32)
            for r, (st, entry) in enumerate(blocks):
                shift = BLK * r - 128 * j
                if shift <= -BLK or shift >= 128:
                    continue
                here = (lane >= max(shift, 0)) & (lane < min(128, shift + BLK))
                moved = st if shift % 128 == 0 else pltpu.roll(st, shift % 128, 1)
                acc = jnp.where(here, moved, acc)
                ids = jnp.where(here, entry, ids)
            lr = acc[0:1, :] + acc[2:3, :] + acc[4:5, :]
            dr = acc[1:2, :] + acc[3:4, :] + acc[5:6, :]
            cols = slice(Q_TILE * half + 128 * j, Q_TILE * half + 128 * (j + 1))
            drow[:, cols] = jnp.broadcast_to(dr, (8, 128))
            lb = jnp.broadcast_to(lr, (8, 128))
            for t in range(4):
                lrow[8 * t : 8 * t + 8, cols] = jnp.where(
                    ids > keyid[8 * t : 8 * t + 8, :], lb, HIDDEN
                )

    def tile(qi, ki):
        qs = pl.ds(pl.multiple_of(qi * Q_TILE, Q_TILE), Q_TILE)
        ks = pl.ds(pl.multiple_of(ki * K_TILE, K_TILE), K_TILE)
        q = qg[pl.ds(qi * 8, 8), 0:ROWS, :].reshape(Q_TILE, WIDTH)
        g = qg[pl.ds(qi * 8, 8), ROWS : 2 * ROWS, :].reshape(Q_TILE, WIDTH)
        k = kv[0, pl.ds(ki * 2, 2), :, :, :].reshape(K_TILE, WIDTH)
        v = kv[1, pl.ds(ki * 2, 2), :, :, :].reshape(K_TILE, WIDTH)
        s = lax.dot_general(k, q, NT, preferred_element_type=F32)
        dp = lax.dot_general(v, g, NT, preferred_element_type=F32)
        lr = lrow[pl.ds(pl.multiple_of(ki * 8, 8), 8), qs]
        bias = jnp.broadcast_to(lr[:, None, :], (8, BLK, Q_TILE)).reshape(K_TILE, Q_TILE)
        p = jnp.exp2(s * TO_EXP2 - bias)
        ds = (p * (dp - drow[0:1, qs])).astype(BF16)
        dv_acc[ks, :] += jnp.dot(p.astype(BF16), g, preferred_element_type=F32)
        dk_acc[ks, :] += jnp.dot(ds, q, preferred_element_type=F32)
        dq_acc[qs, :] += lax.dot_general(ds, k, TN, preferred_element_type=F32)

    dq_cps, sib_cps, dkv_cps = {}, {}, {}
    for i in range(1, 16):
        dx, dy = PLANE[i]
        dq_cps[i] = pltpu.make_async_remote_copy(
            src_ref=dq_send.at[i], dst_ref=dq_recv.at[plane_slot(-dx, -dy)],
            send_sem=dq_ss.at[i], recv_sem=dq_rs.at[plane_slot(-dx, -dy)],
            device_id=plane_dev(i), device_id_type=MESH,
        )
    for s in range(8):
        sib_cps[s] = pltpu.make_async_remote_copy(
            src_ref=sib_send.at[s], dst_ref=sib_recv.at[s],
            send_sem=sib_ss.at[s], recv_sem=sib_rs.at[s],
            device_id=sibling, device_id_type=MESH,
        )
        if s > 0:
            to = line_slot(-LINE[s])
            dkv_cps[s] = pltpu.make_async_remote_copy(
                src_ref=dkv_send.at[s], dst_ref=dkv_recv.at[to],
                send_sem=dkv_ss.at[s], recv_sem=dkv_rs.at[to],
                device_id=line_dev(s), device_id_type=MESH,
            )
    cross = pltpu.make_async_remote_copy(
        src_ref=sib_send.at[1], dst_ref=dkv_cross,
        send_sem=cross_ss, recv_sem=cross_rs,
        device_id=cross_up, device_id_type=MESH,
    )

    def dq_out_half(half):
        for i in range(8 * half, 8 * half + 8):
            if i > 0:
                dq_send[i] = dq_acc[i * ROWS : (i + 1) * ROWS, :].astype(BF16)
                dq_cps[i].start()

    def part(acc, s, h):
        at = s * 2 * ROWS + h * ROWS
        return acc[at : at + ROWS, :]

    def to_sibling(s):
        sib_send[s, 0] = part(dk_acc, s, 1).astype(BF16)
        sib_send[s, 1] = part(dv_acc, s, 1).astype(BF16)
        if s != 1:
            sib_cps[s].start()

    def to_owner(s):
        a, b = part(dk_acc, s, 0), part(dv_acc, s, 0)
        if s != 1:
            sib_cps[s].wait_recv()
            a = a + sib_recv[s, 0].astype(F32)
            b = b + sib_recv[s, 1].astype(F32)
        dkv_send[s, 0] = a.astype(BF16)
        dkv_send[s, 1] = b.astype(BF16)
        dkv_cps[s].start()

    def keys_arrived(group):
        for s in (2 * group, 2 * group + 1):
            if s > 0:
                kz_arrived(s)
                kc_cps[s].start()

    def step(n, carry):
        qi = n // 4
        ki = jnp.where(n < 4, n, 7 - n)

        @pl.when(n == 0)
        def _():
            keys_arrived(0)
            for i in range(1, 8):
                q_arrived(i)
            rows_of(0)

        for group in range(4):

            @pl.when(n == group)
            def _():
                if group > 0:
                    keys_arrived(group)
                for s in (2 * group, 2 * group + 1):
                    kc_cps[s].wait_recv()

        @pl.when(n == 4)
        def _():
            dq_out_half(0)
            for i in range(8, 16):
                q_arrived(i)
            rows_of(1)

        for group in (3, 2, 1):

            @pl.when(n == 8 - group)
            def _():
                for s in (2 * group, 2 * group + 1):
                    to_sibling(s)
                if group < 3:
                    for s in (2 * group + 2, 2 * group + 3):
                        to_owner(s)

        tile(qi, ki)
        return carry

    lax.fori_loop(0, 8, step, 0)

    to_sibling(1)
    cross.start()
    to_owner(1)
    to_sibling(0)
    dq_out_half(1)
    for s in (2, 3):
        to_owner(s)

    total = dq_acc[0:ROWS, :]
    for i in range(1, 16):
        dx, dy = PLANE[i]
        dq_cps[plane_slot(-dx, -dy)].wait_recv()
        total = total + dq_recv[i].astype(F32)
    dq_out[...] = (total * SCALE).astype(BF16)
    a, b = part(dk_acc, 0, 0), part(dv_acc, 0, 0)
    sib_cps[0].wait_recv()
    a, b = a + sib_recv[0, 0].astype(F32), b + sib_recv[0, 1].astype(F32)
    for s in range(1, 8):
        dkv_cps[line_slot(-LINE[s])].wait_recv()
        a, b = a + dkv_recv[s, 0].astype(F32), b + dkv_recv[s, 1].astype(F32)
    cross.wait_recv()
    a, b = a + dkv_cross[0].astype(F32), b + dkv_cross[1].astype(F32)
    dk_out[...] = (a * SCALE).astype(BF16)
    dv_out[...] = b.astype(BF16)

    for group in (q_cps, kz_cps, dq_cps, dkv_cps):
        for cp in group.values():
            cp.wait_send()
    for s in range(8):
        kc_cps[s].wait_send()
        if s != 1:
            sib_cps[s].wait_send()
    cross.wait_send()


def per_device(queries, keys_in, values_in, outputs_saved, out_grad, log_sum, block_table):
    hbm = pl.BlockSpec(memory_space=pl.ANY)
    vmem = pl.BlockSpec(memory_space=pltpu.VMEM)
    smem = pl.BlockSpec(memory_space=pltpu.SMEM)
    dma = pltpu.SemaphoreType.DMA
    out = jax.ShapeDtypeStruct((ROWS, WIDTH), BF16)
    return pl.pallas_call(
        kernel,
        out_shape=(out, out, out),
        in_specs=[hbm, hbm, hbm, hbm, hbm, vmem, smem],
        out_specs=(vmem, vmem, vmem),
        scratch_shapes=[
            pltpu.VMEM((16, CHUNK, WIDTH), BF16),
            pltpu.VMEM((2, 8, 2, ROWS, WIDTH), BF16),
            pltpu.VMEM((ROWS, WIDTH), BF16),
            pltpu.VMEM((16 * ROWS, WIDTH), F32),
            pltpu.VMEM((16 * ROWS, WIDTH), F32),
            pltpu.VMEM((16 * ROWS, WIDTH), F32),
            pltpu.VMEM((32, 16 * ROWS), F32),
            pltpu.VMEM((8, 16 * ROWS), F32),
            pltpu.VMEM((32, 128), jnp.int32),
            pltpu.VMEM((16, ROWS, WIDTH), BF16),
            pltpu.VMEM((16, ROWS, WIDTH), BF16),
            pltpu.VMEM((8, 2, ROWS, WIDTH), BF16),
            pltpu.VMEM((8, 2, ROWS, WIDTH), BF16),
            pltpu.VMEM((8, 2, ROWS, WIDTH), BF16),
            pltpu.VMEM((8, 2, ROWS, WIDTH), BF16),
            pltpu.VMEM((2, ROWS, WIDTH), BF16),
            dma((5,)), dma((16,)), dma((16,)), dma((8,)), dma((8,)), dma((8,)), dma((8,)),
            dma((16,)), dma((16,)), dma((8,)), dma((8,)), dma((8,)), dma((8,)), dma, dma,
        ],
        compiler_params=pltpu.CompilerParams(
            collective_id=0, has_side_effects=True, vmem_limit_bytes=48 << 20
        ),
    )(
        queries, keys_in, values_in, outputs_saved, out_grad,
        log_sum.reshape(1, ROWS), block_table,
    )


def solution(mesh):
    rows = P(("pb", "ka"), None)
    return jax.shard_map(
        per_device,
        mesh=mesh,
        in_specs=(rows, rows, rows, rows, rows, P(("pb", "ka")), P()),
        out_specs=(rows, rows, rows),
        check_vma=False,
    )
```

time: 804 us -> 70.1 us (0.09)
  the two profiles are of different devices: /device:TPU:2 before, /device:TPU:7 now
where the time goes in v1:
time: 70.1 us; the launch traced here: 69.7 us
  Pallas kernels  62 us (88%)
  local copies, waits for them, and re-layouts  7.1 us (10%)
    pallas_call x1, Pallas kernels, per_device(): pl.pallas_call(kernel, out_shape=(out, out, out), in_specs=[hbm, hbm, hbm...  62 us
    unnamed x17, local copies, waits for them, and re-layouts  7.1 us

profile of v1, /device:TPU:7, one launch (start us, length us, event | category | flops | bytes accessed | tf_op | source)
XLA Modules:
  0.0 69.7 jit_solution(10284584360607464533)
XLA Ops:
  0.6 0.0 copy-start.6
  0.6 0.7 copy-done.6
  1.3 0.0 copy-start
  1.3 0.8 %copy-done = bf16[160,128]{1,0:T(8,128)(2,1)S(1)} copy-done((bf16[160,128]{1,0:T(8,128)(2,1)S(1)}, bf16[160,128]{1,0:T(8,128)(2,1)}, u32[]{:S(2)}) %copy-start) | copy-done | bytes 40984
  2.1 0.0 copy-start.1
  2.1 0.8 %copy-done.1 = bf16[160,128]{1,0:T(8,128)(2,1)S(1)} copy-done((bf16[160,128]{1,0:T(8,128)(2,1)S(1)}, bf16[160,128]{1,0:T(8,128)(2,1)}, u32[]{:S(2)}) %copy-start.1) | copy-done | bytes 40984
  2.9 0.0 copy-start.2
  2.9 0.8 %copy-done.2 = bf16[160,128]{1,0:T(8,128)(2,1)S(1)} copy-done((bf16[160,128]{1,0:T(8,128)(2,1)S(1)}, bf16[160,128]{1,0:T(8,128)(2,1)}, u32[]{:S(2)}) %copy-start.2) | copy-done | bytes 40984
  3.6 0.0 copy-start.3
  3.7 0.8 %copy-done.3 = bf16[160,128]{1,0:T(8,128)(2,1)S(1)} copy-done((bf16[160,128]{1,0:T(8,128)(2,1)S(1)}, bf16[160,128]{1,0:T(8,128)(2,1)}, u32[]{:S(2)}) %copy-start.3) | copy-done | bytes 40984
  4.4 0.0 copy-start.4
  4.4 0.8 %copy-done.4 = bf16[160,128]{1,0:T(8,128)(2,1)S(1)} copy-done((bf16[160,128]{1,0:T(8,128)(2,1)S(1)}, bf16[160,128]{1,0:T(8,128)(2,1)}, u32[]{:S(2)}) %copy-start.4) | copy-done | bytes 40984
  5.2 0.0 copy-start.5
  5.2 0.7 copy-done.5
  5.9 62.0 %shard_map.94 = (bf16[160,128]{1,0:T(8,128)(2,1)S(1)}, bf16[160,128]{1,0:T(8,128)(2,1)S(1)}, bf16[160,128]{1,0:T(8,128)(2,1)S(1)}) custom-call(bf16[160,128]{1,0:T(8,128)(2,1)S(1)} %copy-done, bf16[160,128]{1,0:T(8,128)(2,1)S(1)} %copy-done.1, bf16[160,128]{1,0:T(8,128)(2,1)S(1)} %copy-done.2, bf16[160,128]{1,0:T(8,128)(2,1)S(1)} %copy-done.3, ...), custom_call_target="tpu_custom_call" | custom-call | tf_op jit(solution)/shard_map/pallas_call | solution.py:373
  67.8 0.6 copy.13
  68.5 0.6 copy.14
  69.1 0.6 copy.15
Async XLA Ops:
  0.6 0.7 copy-start.6
  1.3 0.8 %copy-start = (bf16[160,128]{1,0:T(8,128)(2,1)S(1)}, bf16[160,128]{1,0:T(8,128)(2,1)}, u32[]{:S(2)}) copy-start(bf16[160,128]{1,0:T(8,128)(2,1)} %q_in.1) | copy-start | bytes 122884
  2.1 0.8 %copy-start.1 = (bf16[160,128]{1,0:T(8,128)(2,1)S(1)}, bf16[160,128]{1,0:T(8,128)(2,1)}, u32[]{:S(2)}) copy-start(bf16[160,128]{1,0:T(8,128)(2,1)} %k_in.1) | copy-start | bytes 122884
  2.9 0.8 %copy-start.2 = (bf16[160,128]{1,0:T(8,128)(2,1)S(1)}, bf16[160,128]{1,0:T(8,128)(2,1)}, u32[]{:S(2)}) copy-start(bf16[160,128]{1,0:T(8,128)(2,1)} %v_in.1) | copy-start | bytes 122884
  3.6 0.8 %copy-start.3 = (bf16[160,128]{1,0:T(8,128)(2,1)S(1)}, bf16[160,128]{1,0:T(8,128)(2,1)}, u32[]{:S(2)}) copy-start(bf16[160,128]{1,0:T(8,128)(2,1)} %o_in.1) | copy-start | bytes 122884
  4.4 0.8 %copy-start.4 = (bf16[160,128]{1,0:T(8,128)(2,1)S(1)}, bf16[160,128]{1,0:T(8,128)(2,1)}, u32[]{:S(2)}) copy-start(bf16[160,128]{1,0:T(8,128)(2,1)} %g_in.1) | copy-start | bytes 122884
  5.2 0.7 copy-start.5

commit v2 on v1

v2 whole, which is shorter than its diff:
```python
import math

import jax
import jax.numpy as jnp
from jax import lax
from jax.experimental import pallas as pl
from jax.experimental.pallas import tpu as pltpu
from jax.sharding import PartitionSpec as P

MESH = pl.DeviceIdType.MESH
F32, BF16 = jnp.float32, jnp.bfloat16
ROWS = 160
BLK = 80
WIDTH = 128
SCALE = 1.0 / math.sqrt(WIDTH)
TO_EXP2 = SCALE * math.log2(math.e)
LOG2E = math.log2(math.e)
HIDDEN = 1e30
CHUNK = 336
PLANE = (
    (0, 0), (1, 0), (3, 0), (0, 1), (0, 3), (2, 0), (0, 2), (1, 1),
    (2, 2), (2, 1), (2, 3), (1, 2), (3, 2), (3, 3), (1, 3), (3, 1),
)
LINE = (0, 1, -1, 2, -2, 3, -3, 4)
Q_TILE, K_TILE = 4 * ROWS, 4 * ROWS
NT = (((1,), (1,)), ((), ()))
TN = (((0,), (0,)), ((), ()))


def place():
    pb, ka = lax.axis_index("pb"), lax.axis_index("ka")
    x, y, z, c = (ka // 2) % 4, ka // 8, (pb // 2) * 2 + ka % 2, pb % 2
    return x, y, z, c


def device(x, y, z, c):
    return ((z // 2) * 2 + c, y * 8 + x * 2 + z % 2)


def storage(x, y, z, c):
    pb, ka = device(x, y, z, c)
    return pb * 32 + ka


def kernel(
    q_in, k_in, v_in, o_in, g_in, l_in, table,
    dq_out, dk_out, dv_out,
    qg, kv, o_own, dq_acc, dk_acc, dv_acc, lrow, drow, keyid,
    dq_send, dq_recv, sib_send, sib_recv, dkv_send, dkv_recv, relay_recv, dkv_cross,
    local_sem, q_ss, q_rs, kz_ss, kz_rs, kc_ss, kc_rs,
    dq_ss, dq_rs, sib_ss, sib_rs, dkv_ss, dkv_rs, cross_ss, cross_rs,
):
    x, y, z, c = place()
    other = 1 - c

    def plane_dev(i, sign):
        dx, dy = PLANE[i]
        return device((x + sign * dx + 4) % 4, (y + sign * dy + 4) % 4, z, c)

    def line_dev(dz, core):
        return device(x, y, (z + dz + 8) % 8, core)

    sibling = device(x, y, z, other)
    partners = [plane_dev(i, 1) for i in range(1, 16)]
    partners += [line_dev(dz, c) for dz in (1, -1, 2, -2)]
    partners += [sibling, line_dev(1, other), line_dev(-1, other)]
    barrier = pltpu.get_barrier_semaphore()
    for p in partners:
        pl.semaphore_signal(barrier, inc=1, device_id=p, device_id_type=MESH)

    loads = [
        pltpu.make_async_copy(g_in, qg.at[0, pl.ds(ROWS, ROWS)], local_sem.at[0]),
        pltpu.make_async_copy(o_in, o_own, local_sem.at[1]),
        pltpu.make_async_copy(q_in, qg.at[0, pl.ds(0, ROWS)], local_sem.at[2]),
        pltpu.make_async_copy(k_in, kv.at[0, 0, 0], local_sem.at[3]),
        pltpu.make_async_copy(v_in, kv.at[1, 0, 0], local_sem.at[4]),
    ]
    for cp in loads:
        cp.start()
    dq_acc[...] = jnp.zeros_like(dq_acc)
    dk_acc[...] = jnp.zeros_like(dk_acc)
    dv_acc[...] = jnp.zeros_like(dv_acc)
    for cp in loads:
        cp.wait()

    q0, g0 = qg[0, 0:ROWS, :], qg[0, ROWS : 2 * ROWS, :]
    k0, v0 = kv[0, 0, 0], kv[1, 0, 0]
    prod = g0.astype(F32) * o_own[...].astype(F32)
    high = prod.astype(BF16)
    low = (prod - high.astype(F32)).astype(BF16)
    ones = jnp.ones((8, WIDTH), BF16)
    delta8 = lax.dot_general(ones, high, NT, preferred_element_type=F32)
    delta8 += lax.dot_general(ones, low, NT, preferred_element_type=F32)
    delta = delta8[0:1, :]
    lse = l_in[...] * LOG2E
    sub = lax.broadcasted_iota(jnp.int32, (8, ROWS), 0)
    both = jnp.where(sub % 2 == 0, lse, delta)
    p1 = both.astype(BF16).astype(F32)
    p2 = (both - p1).astype(BF16).astype(F32)
    p3 = both - p1 - p2
    pieces = jnp.where(sub < 2, p1, jnp.where(sub < 4, p2, jnp.where(sub < 6, p3, 0.0)))
    wide = jnp.concatenate([pieces, jnp.zeros((8, 256 - ROWS), F32)], axis=1)
    first, rest = wide[:, 0:128], wide[:, 128:256]
    lane = lax.broadcasted_iota(jnp.int32, (8, 128), 1)
    second = jnp.where(
        lane < 48, pltpu.roll(first, 48, 1), pltpu.roll(rest, 48, 1)
    )
    keep = lane < BLK
    stats = jnp.concatenate(
        [jnp.where(keep, first, 0.0), jnp.where(keep, second, 0.0)], axis=0
    )
    qg[0, 2 * ROWS : CHUNK, :] = stats.astype(BF16)

    q_cps = {
        i: pltpu.make_async_remote_copy(
            src_ref=qg.at[0], dst_ref=qg.at[i],
            send_sem=q_ss.at[i], recv_sem=q_rs.at[i],
            device_id=plane_dev(i, -1), device_id_type=MESH,
        )
        for i in range(1, 16)
    }
    kz_cps = {}
    for s in range(1, 7):
        held, to = (0, -LINE[s]) if s < 5 else (s - 2, -1 if s == 5 else 1)
        kz_cps[s] = pltpu.make_async_remote_copy(
            src_ref=kv.at[:, held, 0], dst_ref=kv.at[:, s, 0],
            send_sem=kz_ss.at[s], recv_sem=kz_rs.at[s],
            device_id=line_dev(to, c), device_id_type=MESH,
        )
    for s, (part, held, to) in {7: (0, 3, -2), 8: (1, 4, 2)}.items():
        kz_cps[s] = pltpu.make_async_remote_copy(
            src_ref=kv.at[part, held, 0], dst_ref=kv.at[part, 7, 0],
            send_sem=kz_ss.at[s], recv_sem=kz_rs.at[s],
            device_id=line_dev(to, c), device_id_type=MESH,
        )
    kc_cps = [
        pltpu.make_async_remote_copy(
            src_ref=kv.at[:, s, 0], dst_ref=kv.at[:, s, 1],
            send_sem=kc_ss.at[s], recv_sem=kc_rs.at[s],
            device_id=sibling, device_id_type=MESH,
        )
        for s in range(8)
    ]

    pl.semaphore_wait(barrier, len(partners))
    for cp in (
        kz_cps[1], kz_cps[2], q_cps[1], q_cps[2], q_cps[3], q_cps[4], kc_cps[0],
        kz_cps[3], kz_cps[4], q_cps[5], q_cps[6], q_cps[7],
    ):
        cp.start()

    row = lax.broadcasted_iota(jnp.int32, (ROWS, ROWS), 0)
    col = lax.broadcasted_iota(jnp.int32, (ROWS, ROWS), 1)
    seen = (row <= col) & ((row >= BLK) == (col >= BLK))
    s0 = lax.dot_general(k0, q0, NT, preferred_element_type=F32)
    e0 = jnp.exp2(jnp.where(seen, s0 * TO_EXP2 - lse, -HIDDEN))
    dp0 = lax.dot_general(v0, g0, NT, preferred_element_type=F32)
    ds0 = (e0 * (dp0 - delta)).astype(BF16)
    dq_acc[0:ROWS, :] = lax.dot_general(ds0, k0, TN, preferred_element_type=F32)
    dk_acc[0:ROWS, :] = jnp.dot(ds0, q0, preferred_element_type=F32)
    dv_acc[0:ROWS, :] = jnp.dot(e0.astype(BF16), g0, preferred_element_type=F32)

    for r in range(32):
        s, h, b = r // 4, (r % 4) // 2, r % 2
        at = storage(x, y, (z + LINE[s] + 8) % 8, c if h == 0 else other) * 2 + b
        keyid[r : r + 1, :] = jnp.full((1, 128), table[at], jnp.int32)

    def rows_of(t):
        blocks = []
        for i in range(4 * t, 4 * t + 4):
            st = qg[i, 2 * ROWS : CHUNK, :].astype(F32)
            dx, dy = PLANE[i]
            at = storage((x + dx) % 4, (y + dy) % 4, z, c) * 2
            blocks += [(st[0:8, :], table[at]), (st[8:16, :], table[at + 1])]
        for j in range(5):
            acc = jnp.zeros((8, 128), F32)
            ids = jnp.zeros((8, 128), jnp.int32)
            for r, (st, entry) in enumerate(blocks):
                shift = BLK * r - 128 * j
                if shift <= -BLK or shift >= 128:
                    continue
                here = (lane >= max(shift, 0)) & (lane < min(128, shift + BLK))
                moved = st if shift % 128 == 0 else pltpu.roll(st, shift % 128, 1)
                acc = jnp.where(here, moved, acc)
                ids = jnp.where(here, entry, ids)
            lr = acc[0:1, :] + acc[2:3, :] + acc[4:5, :]
            dr = acc[1:2, :] + acc[3:4, :] + acc[5:6, :]
            cols = slice(Q_TILE * t + 128 * j, Q_TILE * t + 128 * (j + 1))
            drow[:, cols] = jnp.broadcast_to(dr, (8, 128))
            lb = jnp.broadcast_to(lr, (8, 128))
            for u in range(4):
                lrow[8 * u : 8 * u + 8, cols] = jnp.where(
                    ids > keyid[8 * u : 8 * u + 8, :], lb, HIDDEN
                )

    def tile(qi, ki):
        qs = pl.ds(pl.multiple_of(qi * Q_TILE, Q_TILE), Q_TILE)
        ks = pl.ds(pl.multiple_of(ki * K_TILE, K_TILE), K_TILE)
        q = qg[pl.ds(qi * 4, 4), 0:ROWS, :].reshape(Q_TILE, WIDTH)
        g = qg[pl.ds(qi * 4, 4), ROWS : 2 * ROWS, :].reshape(Q_TILE, WIDTH)
        k = kv[0, pl.ds(ki * 2, 2), :, :, :].reshape(K_TILE, WIDTH)
        v = kv[1, pl.ds(ki * 2, 2), :, :, :].reshape(K_TILE, WIDTH)
        s = lax.dot_general(k, q, NT, preferred_element_type=F32)
        dp = lax.dot_general(v, g, NT, preferred_element_type=F32)
        lr = lrow[pl.ds(pl.multiple_of(ki * 8, 8), 8), qs]
        bias = jnp.broadcast_to(lr[:, None, :], (8, BLK, Q_TILE)).reshape(K_TILE, Q_TILE)
        p = jnp.exp2(s * TO_EXP2 - bias)
        ds = (p * (dp - drow[0:1, qs])).astype(BF16)
        dv_acc[ks, :] += jnp.dot(p.astype(BF16), g, preferred_element_type=F32)
        dk_acc[ks, :] += jnp.dot(ds, q, preferred_element_type=F32)
        dq_acc[qs, :] += lax.dot_general(ds, k, TN, preferred_element_type=F32)

    dq_cps = {
        i: pltpu.make_async_remote_copy(
            src_ref=dq_send.at[i], dst_ref=dq_recv.at[i],
            send_sem=dq_ss.at[i], recv_sem=dq_rs.at[i],
            device_id=plane_dev(i, 1), device_id_type=MESH,
        )
        for i in range(1, 16)
    }
    sib_cps = {
        s: pltpu.make_async_remote_copy(
            src_ref=sib_send.at[s], dst_ref=sib_recv.at[s],
            send_sem=sib_ss.at[s], recv_sem=sib_rs.at[s],
            device_id=sibling, device_id_type=MESH,
        )
        for s in (0, 2, 3, 4, 5, 6, 7)
    }
    dkv_cps = {
        s: pltpu.make_async_remote_copy(
            src_ref=dkv_send.at[s], dst_ref=dkv_recv.at[s] if s < 5 else relay_recv.at[s - 5],
            send_sem=dkv_ss.at[s], recv_sem=dkv_rs.at[s],
            device_id=line_dev(LINE[s] if s < 5 else (1 if s == 5 else -1), c),
            device_id_type=MESH,
        )
        for s in range(1, 7)
    }
    for s, (part, to) in {7: (0, 2), 8: (1, -2)}.items():
        dkv_cps[s] = pltpu.make_async_remote_copy(
            src_ref=dkv_send.at[7, part], dst_ref=relay_recv.at[2, part],
            send_sem=dkv_ss.at[s], recv_sem=dkv_rs.at[s],
            device_id=line_dev(to, c), device_id_type=MESH,
        )
    cross = pltpu.make_async_remote_copy(
        src_ref=sib_send.at[1], dst_ref=dkv_cross,
        send_sem=cross_ss, recv_sem=cross_rs,
        device_id=line_dev(1, other), device_id_type=MESH,
    )

    def queries_out(t):
        for i in range(4 * t, 4 * t + 4):
            if i > 0:
                dq_send[i] = dq_acc[i * ROWS : (i + 1) * ROWS, :].astype(BF16)
                dq_cps[i].start()

    def part(acc, s, h):
        at = s * 2 * ROWS + h * ROWS
        return acc[at : at + ROWS, :]

    def to_sibling(s):
        sib_send[s, 0] = part(dk_acc, s, 1).astype(BF16)
        sib_send[s, 1] = part(dv_acc, s, 1).astype(BF16)
        (cross if s == 1 else sib_cps[s]).start()

    def to_owner(s):
        a, b = part(dk_acc, s, 0), part(dv_acc, s, 0)
        if s != 1:
            sib_cps[s].wait_recv()
            a = a + sib_recv[s, 0].astype(F32)
            b = b + sib_recv[s, 1].astype(F32)
        if s in (3, 4):
            dkv_cps[s + 2].wait_recv()
            dkv_cps[s + 4].wait_recv()
            a = a + relay_recv[s - 3, 0].astype(F32)
            b = b + relay_recv[s - 3, 1].astype(F32)
            if s == 3:
                a = a + relay_recv[2, 0].astype(F32)
            else:
                b = b + relay_recv[2, 1].astype(F32)
        dkv_send[s, 0] = a.astype(BF16)
        dkv_send[s, 1] = b.astype(BF16)
        dkv_cps[s].start()
        if s == 7:
            dkv_cps[8].start()

    def before(n):
        if n == 0:
            for s in (1, 2):
                kz_cps[s].wait_recv()
                kc_cps[s].start()
            for i in (1, 2, 3, 4):
                q_cps[i].wait_recv()
            for i in range(15, 7, -1):
                q_cps[i].start()
            rows_of(0)
            kc_cps[0].wait_recv()
            kc_cps[1].wait_recv()
        if n == 1:
            for s in (3, 4):
                kz_cps[s].wait_recv()
                kz_cps[s + 2].start()
                kz_cps[s + 4].start()
                kc_cps[s].start()
            for i in (5, 6, 7):
                q_cps[i].wait_recv()
            rows_of(1)
        if n == 2:
            kc_cps[2].wait_recv()
            kc_cps[3].wait_recv()
        if n == 4:
            for s in (5, 6):
                kz_cps[s].wait_recv()
                kc_cps[s].start()
            kc_cps[4].wait_recv()
            kc_cps[5].wait_recv()
        if n == 6:
            kz_cps[7].wait_recv()
            kz_cps[8].wait_recv()
            kc_cps[7].start()
            kc_cps[6].wait_recv()
            kc_cps[7].wait_recv()
        if n == 8:
            queries_out(0)
            queries_out(1)
            for i in (8, 9, 10, 11):
                q_cps[i].wait_recv()
            rows_of(2)
        if n == 9:
            for i in (12, 13, 14, 15):
                q_cps[i].wait_recv()
            rows_of(3)
        if n == 10:
            to_sibling(6)
            to_sibling(7)
        if n == 11:
            to_owner(6)
            to_owner(7)
        if n == 12:
            to_sibling(5)
            to_sibling(4)
        if n == 13:
            to_owner(5)
        if n == 14:
            queries_out(2)
        if n == 15:
            to_sibling(3)
            to_sibling(2)

    def step(n, carry):
        qi = jnp.where(n < 8, n % 2, jnp.where(n < 12, 2 + n % 2, 2 + (n - 12) // 2))
        ki = jnp.where(n < 8, n // 2, jnp.where(n < 12, 3 - (n - 8) // 2, 1 - n % 2))
        for hook in (0, 1, 2, 4, 6, 8, 9, 10, 11, 12, 13, 14, 15):
            pl.when(n == hook)(lambda hook=hook: before(hook))
        tile(qi, ki)
        return carry

    lax.fori_loop(0, 16, step, 0)

    to_sibling(1)
    to_owner(1)
    to_sibling(0)
    queries_out(3)
    for s in (4, 2, 3):
        to_owner(s)

    a, b = part(dk_acc, 0, 0), part(dv_acc, 0, 0)
    sib_cps[0].wait_recv()
    a, b = a + sib_recv[0, 0].astype(F32), b + sib_recv[0, 1].astype(F32)
    total = dq_acc[0:ROWS, :]
    for i in range(1, 16):
        dq_cps[i].wait_recv()
        total = total + dq_recv[i].astype(F32)
    dq_out[...] = (total * SCALE).astype(BF16)
    cross.wait_recv()
    a, b = a + dkv_cross[0].astype(F32), b + dkv_cross[1].astype(F32)
    for s in range(1, 5):
        dkv_cps[s].wait_recv()
        a, b = a + dkv_recv[s, 0].astype(F32), b + dkv_recv[s, 1].astype(F32)
    dk_out[...] = (a * SCALE).astype(BF16)
    dv_out[...] = b.astype(BF16)

    for group in (q_cps, kz_cps, dq_cps, dkv_cps, sib_cps):
        for cp in group.values():
            cp.wait_send()
    for cp in kc_cps:
        cp.wait_send()
    cross.wait_send()


def per_device(queries, keys_in, values_in, outputs_saved, out_grad, log_sum, block_table):
    hbm = pl.BlockSpec(memory_space=pl.ANY)
    vmem = pl.BlockSpec(memory_space=pltpu.VMEM)
    smem = pl.BlockSpec(memory_space=pltpu.SMEM)
    dma = pltpu.SemaphoreType.DMA
    out = jax.ShapeDtypeStruct((ROWS, WIDTH), BF16)
    return pl.pallas_call(
        kernel,
        out_shape=(out, out, out),
        in_specs=[hbm, hbm, hbm, hbm, hbm, vmem, smem],
        out_specs=(vmem, vmem, vmem),
        scratch_shapes=[
            pltpu.VMEM((16, CHUNK, WIDTH), BF16),
            pltpu.VMEM((2, 8, 2, ROWS, WIDTH), BF16),
            pltpu.VMEM((ROWS, WIDTH), BF16),
            pltpu.VMEM((16 * ROWS, WIDTH), F32),
            pltpu.VMEM((16 * ROWS, WIDTH), F32),
            pltpu.VMEM((16 * ROWS, WIDTH), F32),
            pltpu.VMEM((32, 16 * ROWS), F32),
            pltpu.VMEM((8, 16 * ROWS), F32),
            pltpu.VMEM((32, 128), jnp.int32),
            pltpu.VMEM((16, ROWS, WIDTH), BF16),
            pltpu.VMEM((16, ROWS, WIDTH), BF16),
            pltpu.VMEM((8, 2, ROWS, WIDTH), BF16),
            pltpu.VMEM((8, 2, ROWS, WIDTH), BF16),
            pltpu.VMEM((8, 2, ROWS, WIDTH), BF16),
            pltpu.VMEM((5, 2, ROWS, WIDTH), BF16),
            pltpu.VMEM((3, 2, ROWS, WIDTH), BF16),
            pltpu.VMEM((2, ROWS, WIDTH), BF16),
            dma((5,)), dma((16,)), dma((16,)), dma((9,)), dma((9,)), dma((8,)), dma((8,)),
            dma((16,)), dma((16,)), dma((8,)), dma((8,)), dma((9,)), dma((9,)), dma, dma,
        ],
        compiler_params=pltpu.CompilerParams(
            collective_id=0, has_side_effects=True, vmem_limit_bytes=60 << 20
        ),
    )(
        queries, keys_in, values_in, outputs_saved, out_grad,
        log_sum.reshape(1, ROWS), block_table,
    )


def solution(mesh):
    rows = P(("pb", "ka"), None)
    return jax.shard_map(
        per_device,
        mesh=mesh,
        in_specs=(rows, rows, rows, rows, rows, P(("pb", "ka")), P()),
        out_specs=(rows, rows, rows),
        check_vma=False,
    )
```

time: 70.1 us -> 58.8 us (0.84)
  the two profiles are of different devices: /device:TPU:7 before, /device:TPU:12 now
where the time goes in v2:
time: 58.8 us; the launch traced here: 58.5 us
  Pallas kernels  55 us (94%)
  local copies, waits for them, and re-layouts  2.82 us (5%)
  between operations  0.65 us (1%)
    pallas_call x1, Pallas kernels, per_device(): pl.pallas_call(kernel, out_shape=(out, out, out), in_specs=[hbm, hbm, hbm...  55 us
    unnamed x7, local copies, waits for them, and re-layouts  2.82 us

profile of v2, /device:TPU:12, one launch (start us, length us, event | category | flops | bytes accessed | tf_op | source)
XLA Modules:
  0.0 58.5 jit_solution(1109798792550266666)
XLA Ops:
  0.6 55.0 %shard_map.94 = (bf16[160,128]{1,0:T(8,128)(2,1)}, bf16[160,128]{1,0:T(8,128)(2,1)}, bf16[160,128]{1,0:T(8,128)(2,1)}) custom-call(bf16[160,128]{1,0:T(8,128)(2,1)} %q_in.1, bf16[160,128]{1,0:T(8,128)(2,1)} %k_in.1, bf16[160,128]{1,0:T(8,128)(2,1)} %v_in.1, bf16[160,128]{1,0:T(8,128)(2,1)} %o_in.1, bf16[160,128]{1,0:T(8,128)(2,1)} %g_in.1, ...), custom_call_target="tpu_custom_call" | custom-call | tf_op jit(solution)/shard_map/pallas_call | solution.py:396
  55.6 0.0 copy-start.1
  55.6 1.4 %copy.13 = bf16[160,128]{1,0:T(8,128)(2,1)} copy(bf16[160,128]{1,0:T(8,128)(2,1)} %get-tuple-element.6) | data formatting | bytes 81920
  57.0 0.0 copy-done.1
  57.0 0.0 copy-start
  57.1 0.6 %copy.14 = bf16[160,128]{1,0:T(8,128)(2,1)} copy(bf16[160,128]{1,0:T(8,128)(2,1)S(1)} %copy-done.1) | data formatting | bytes 81920
  57.7 0.2 copy-done
  57.8 0.6 %copy.15 = bf16[160,128]{1,0:T(8,128)(2,1)} copy(bf16[160,128]{1,0:T(8,128)(2,1)S(1)} %copy-done) | data formatting | bytes 81920
Async XLA Ops:
  55.6 1.4 %copy-start.1 = (bf16[160,128]{1,0:T(8,128)(2,1)S(1)}, bf16[160,128]{1,0:T(8,128)(2,1)}, u32[]{:S(2)}) copy-start(bf16[160,128]{1,0:T(8,128)(2,1)} %get-tuple-element.7) | copy-start | bytes 122884
  57.0 0.8 %copy-start = (bf16[160,128]{1,0:T(8,128)(2,1)S(1)}, bf16[160,128]{1,0:T(8,128)(2,1)}, u32[]{:S(2)}) copy-start(bf16[160,128]{1,0:T(8,128)(2,1)} %get-tuple-element.8) | copy-start | bytes 122884

commit v3 on v2

v3 whole, which is shorter than its diff:
```python
import math

import jax
import jax.numpy as jnp
from jax import lax
from jax.experimental import pallas as pl
from jax.experimental.pallas import tpu as pltpu
from jax.sharding import PartitionSpec as P

MESH = pl.DeviceIdType.MESH
F32, BF16 = jnp.float32, jnp.bfloat16
ROWS = 160
BLK = 80
WIDTH = 128
SCALE = 1.0 / math.sqrt(WIDTH)
TO_EXP2 = SCALE * math.log2(math.e)
LOG2E = math.log2(math.e)
HIDDEN = 1e30
CHUNK = 336
PLANE = (
    (0, 0), (1, 0), (3, 0), (0, 1), (0, 3), (2, 0), (0, 2), (1, 1),
    (2, 2), (2, 1), (2, 3), (1, 2), (3, 2), (3, 3), (1, 3), (3, 1),
)
LINE = (
    (0, 0), (1, 0), (-1, 0), (0, 1), (1, 1), (-1, 1), (2, 0), (-2, 0),
    (2, 1), (-2, 1), (3, 0), (-3, 0), (3, 1), (-3, 1), (4, 0), (4, 1),
)
MINE = {dz: LINE.index((dz, 0)) for dz in (0, 1, -1, 2, -2, 3, -3, 4)}
THEIRS = {dz: LINE.index((dz, 1)) for dz in (0, 1, -1, 2, -2, 3, -3, 4)}
TILES = (
    (0, 0), (0, 1), (1, 1), (1, 0), (1, 2), (0, 2), (0, 3), (1, 3),
    (2, 3), (3, 3), (3, 2), (2, 2), (2, 1), (2, 0), (3, 1), (3, 0),
)
Q_TILE, K_TILE = 4 * ROWS, 4 * ROWS
NT = (((1,), (1,)), ((), ()))
TN = (((0,), (0,)), ((), ()))


def pick(values, n):
    out = values[0]
    for i in range(1, len(values)):
        out = jnp.where(n == i, values[i], out)
    return out


def place():
    pb, ka = lax.axis_index("pb"), lax.axis_index("ka")
    x, y, z, c = (ka // 2) % 4, ka // 8, (pb // 2) * 2 + ka % 2, pb % 2
    return x, y, z, c


def device(x, y, z, c):
    return ((z // 2) * 2 + c, y * 8 + x * 2 + z % 2)


def storage(x, y, z, c):
    pb, ka = device(x, y, z, c)
    return pb * 32 + ka


def kernel(
    q_in, k_in, v_in, o_in, g_in, l_in, table,
    dq_out, dk_out, dv_out,
    qg, kv, o_own, dq_acc, dk_acc, dv_acc, lrow, drow, keyid,
    dq_send, dq_recv, sib_send, sib_recv, dkv_send, dkv_recv,
    local_sem, q_ss, q_rs, kz_ss, kz_rs, kc_ss, kc_rs,
    dq_ss, dq_rs, sib_ss, sib_rs, dkv_ss, dkv_rs,
):
    x, y, z, c = place()
    other = 1 - c

    def plane_dev(i, sign):
        dx, dy = PLANE[i]
        return device((x + sign * dx + 4) % 4, (y + sign * dy + 4) % 4, z, c)

    def line_dev(dz, core):
        return device(x, y, (z + dz + 8) % 8, core)

    sibling = device(x, y, z, other)
    partners = [plane_dev(i, 1) for i in range(1, 16)]
    partners += [line_dev(dz, c) for dz in (1, -1, 2, -2)] + [sibling]
    barrier = pltpu.get_barrier_semaphore()
    for p in partners:
        pl.semaphore_signal(barrier, inc=1, device_id=p, device_id_type=MESH)

    loads = [
        pltpu.make_async_copy(g_in, qg.at[0, pl.ds(ROWS, ROWS)], local_sem.at[0]),
        pltpu.make_async_copy(o_in, o_own, local_sem.at[1]),
        pltpu.make_async_copy(q_in, qg.at[0, pl.ds(0, ROWS)], local_sem.at[2]),
        pltpu.make_async_copy(k_in, kv.at[0, 0], local_sem.at[3]),
        pltpu.make_async_copy(v_in, kv.at[1, 0], local_sem.at[4]),
    ]
    for cp in loads:
        cp.start()
    dq_acc[...] = jnp.zeros_like(dq_acc)
    dk_acc[...] = jnp.zeros_like(dk_acc)
    dv_acc[...] = jnp.zeros_like(dv_acc)
    for cp in loads:
        cp.wait()

    q0, g0 = qg[0, 0:ROWS, :], qg[0, ROWS : 2 * ROWS, :]
    k0, v0 = kv[0, 0], kv[1, 0]
    prod = g0.astype(F32) * o_own[...].astype(F32)
    high = prod.astype(BF16)
    low = (prod - high.astype(F32)).astype(BF16)
    ones = jnp.ones((8, WIDTH), BF16)
    delta8 = lax.dot_general(ones, high, NT, preferred_element_type=F32)
    delta8 += lax.dot_general(ones, low, NT, preferred_element_type=F32)
    delta = delta8[0:1, :]
    lse = l_in[...] * LOG2E
    sub = lax.broadcasted_iota(jnp.int32, (8, ROWS), 0)
    both = jnp.where(sub % 2 == 0, lse, delta)
    p1 = both.astype(BF16).astype(F32)
    p2 = (both - p1).astype(BF16).astype(F32)
    p3 = both - p1 - p2
    pieces = jnp.where(sub < 2, p1, jnp.where(sub < 4, p2, jnp.where(sub < 6, p3, 0.0)))
    wide = jnp.concatenate([pieces, jnp.zeros((8, 256 - ROWS), F32)], axis=1)
    first, rest = wide[:, 0:128], wide[:, 128:256]
    lane = lax.broadcasted_iota(jnp.int32, (8, 128), 1)
    second = jnp.where(
        lane < 48, pltpu.roll(first, 48, 1), pltpu.roll(rest, 48, 1)
    )
    keep = lane < BLK
    stats = jnp.concatenate(
        [jnp.where(keep, first, 0.0), jnp.where(keep, second, 0.0)], axis=0
    )
    qg[0, 2 * ROWS : CHUNK, :] = stats.astype(BF16)

    def q_copy(i, held, dx, dy, sem, rows=(0, CHUNK)):
        return pltpu.make_async_remote_copy(
            src_ref=qg.at[held, pl.ds(*rows)], dst_ref=qg.at[i, pl.ds(*rows)],
            send_sem=q_ss.at[sem], recv_sem=q_rs.at[sem],
            device_id=device((x - dx + 4) % 4, (y - dy + 4) % 4, z, c), device_id_type=MESH,
        )

    at = {offset: i for i, offset in enumerate(PLANE)}
    q_cps = {}
    for offset in ((1, 0), (3, 0), (0, 1), (0, 3), (2, 0), (0, 2)):
        q_cps[at[offset]] = q_copy(at[offset], 0, *offset, at[offset])
    for dx, dy in ((1, 1), (3, 3), (1, 2), (3, 2)):
        q_cps[at[dx, dy]] = q_copy(at[dx, dy], at[0, dy], dx, 0, at[dx, dy])
    for dx, dy in ((1, 3), (3, 1), (2, 1), (2, 3)):
        q_cps[at[dx, dy]] = q_copy(at[dx, dy], at[dx, 0], 0, dy, at[dx, dy])
    far = at[2, 2]
    q_cps[far] = q_copy(far, at[0, 2], 2, 0, far, (0, 176))
    q_cps[16] = q_copy(far, at[2, 0], 0, 2, 16, (176, CHUNK - 176))

    kz_cps = {}
    for dz, (held, step) in {
        1: (0, 1), -1: (0, -1), 2: (0, 2), -2: (0, -2), 3: (1, 2), -3: (-1, -2),
    }.items():
        kz_cps[dz] = pltpu.make_async_remote_copy(
            src_ref=kv.at[:, MINE[held]], dst_ref=kv.at[:, MINE[dz]],
            send_sem=kz_ss.at[dz + 3], recv_sem=kz_rs.at[dz + 3],
            device_id=line_dev(-step, c), device_id_type=MESH,
        )
    for name, part, step in ((4, 0, 2), (5, 1, -2)):
        kz_cps[name] = pltpu.make_async_remote_copy(
            src_ref=kv.at[part, MINE[step]], dst_ref=kv.at[part, MINE[4]],
            send_sem=kz_ss.at[name + 3], recv_sem=kz_rs.at[name + 3],
            device_id=line_dev(-step, c), device_id_type=MESH,
        )
    kc_cps = {
        dz: pltpu.make_async_remote_copy(
            src_ref=kv.at[:, MINE[dz]], dst_ref=kv.at[:, THEIRS[dz]],
            send_sem=kc_ss.at[dz + 3], recv_sem=kc_rs.at[dz + 3],
            device_id=sibling, device_id_type=MESH,
        )
        for dz in MINE
    }

    pl.semaphore_wait(barrier, len(partners))
    for cp in (
        kz_cps[1], kz_cps[-1], q_cps[at[1, 0]], q_cps[at[3, 0]], q_cps[at[0, 1]], q_cps[at[0, 3]],
        kc_cps[0], kz_cps[2], kz_cps[-2], q_cps[at[2, 0]], q_cps[at[0, 2]],
    ):
        cp.start()

    row = lax.broadcasted_iota(jnp.int32, (ROWS, ROWS), 0)
    col = lax.broadcasted_iota(jnp.int32, (ROWS, ROWS), 1)
    seen = (row <= col) & ((row >= BLK) == (col >= BLK))
    s0 = lax.dot_general(k0, q0, NT, preferred_element_type=F32)
    e0 = jnp.exp2(jnp.where(seen, s0 * TO_EXP2 - lse, -HIDDEN))
    dp0 = lax.dot_general(v0, g0, NT, preferred_element_type=F32)
    ds0 = (e0 * (dp0 - delta)).astype(BF16)
    dq_acc[0:ROWS, :] = lax.dot_general(ds0, k0, TN, preferred_element_type=F32)
    dk_acc[0:ROWS, :] = jnp.dot(ds0, q0, preferred_element_type=F32)
    dv_acc[0:ROWS, :] = jnp.dot(e0.astype(BF16), g0, preferred_element_type=F32)

    for r in range(32):
        dz, h = LINE[r // 2]
        entry = storage(x, y, (z + dz + 8) % 8, c if h == 0 else other) * 2 + r % 2
        keyid[r : r + 1, :] = jnp.full((1, 128), table[entry], jnp.int32)

    def rows_of(t):
        blocks = []
        for i in range(4 * t, 4 * t + 4):
            st = qg[i, 2 * ROWS : CHUNK, :].astype(F32)
            dx, dy = PLANE[i]
            entry = storage((x + dx) % 4, (y + dy) % 4, z, c) * 2
            blocks += [(st[0:8, :], table[entry]), (st[8:16, :], table[entry + 1])]
        for j in range(5):
            acc = jnp.zeros((8, 128), F32)
            ids = jnp.zeros((8, 128), jnp.int32)
            for r, (st, entry) in enumerate(blocks):
                shift = BLK * r - 128 * j
                if shift <= -BLK or shift >= 128:
                    continue
                here = (lane >= max(shift, 0)) & (lane < min(128, shift + BLK))
                moved = st if shift % 128 == 0 else pltpu.roll(st, shift % 128, 1)
                acc = jnp.where(here, moved, acc)
                ids = jnp.where(here, entry, ids)
            lr = acc[0:1, :] + acc[2:3, :] + acc[4:5, :]
            dr = acc[1:2, :] + acc[3:4, :] + acc[5:6, :]
            cols = slice(Q_TILE * t + 128 * j, Q_TILE * t + 128 * (j + 1))
            drow[:, cols] = jnp.broadcast_to(dr, (8, 128))
            lb = jnp.broadcast_to(lr, (8, 128))
            for u in range(4):
                lrow[8 * u : 8 * u + 8, cols] = jnp.where(
                    ids > keyid[8 * u : 8 * u + 8, :], lb, HIDDEN
                )

    def tile(qi, ki):
        qs = pl.ds(pl.multiple_of(qi * Q_TILE, Q_TILE), Q_TILE)
        ks = pl.ds(pl.multiple_of(ki * K_TILE, K_TILE), K_TILE)
        q = qg[pl.ds(qi * 4, 4), 0:ROWS, :].reshape(Q_TILE, WIDTH)
        g = qg[pl.ds(qi * 4, 4), ROWS : 2 * ROWS, :].reshape(Q_TILE, WIDTH)
        k = kv[0, pl.ds(ki * 4, 4), :, :].reshape(K_TILE, WIDTH)
        v = kv[1, pl.ds(ki * 4, 4), :, :].reshape(K_TILE, WIDTH)
        s = lax.dot_general(k, q, NT, preferred_element_type=F32)
        dp = lax.dot_general(v, g, NT, preferred_element_type=F32)
        lr = lrow[pl.ds(pl.multiple_of(ki * 8, 8), 8), qs]
        bias = jnp.broadcast_to(lr[:, None, :], (8, BLK, Q_TILE)).reshape(K_TILE, Q_TILE)
        p = jnp.exp2(s * TO_EXP2 - bias)
        ds = (p * (dp - drow[0:1, qs])).astype(BF16)
        dv_acc[ks, :] += jnp.dot(p.astype(BF16), g, preferred_element_type=F32)
        dk_acc[ks, :] += jnp.dot(ds, q, preferred_element_type=F32)
        dq_acc[qs, :] += lax.dot_general(ds, k, TN, preferred_element_type=F32)

    dq_cps = {
        i: pltpu.make_async_remote_copy(
            src_ref=dq_send.at[i], dst_ref=dq_recv.at[i],
            send_sem=dq_ss.at[i], recv_sem=dq_rs.at[i],
            device_id=plane_dev(i, 1), device_id_type=MESH,
        )
        for i in range(1, 16)
    }
    sib_cps = {
        dz: pltpu.make_async_remote_copy(
            src_ref=sib_send.at[dz + 3], dst_ref=sib_recv.at[dz + 3],
            send_sem=sib_ss.at[dz + 3], recv_sem=sib_rs.at[dz + 3],
            device_id=sibling, device_id_type=MESH,
        )
        for dz in MINE
    }
    dkv_cps = {
        dz: pltpu.make_async_remote_copy(
            src_ref=dkv_send.at[dz + 3], dst_ref=dkv_recv.at[dz + 3],
            send_sem=dkv_ss.at[dz + 3], recv_sem=dkv_rs.at[dz + 3],
            device_id=line_dev(step, c), device_id_type=MESH,
        )
        for dz, step in {1: 1, -1: -1, 2: 2, -2: -2, 3: 2, -3: -2}.items()
    }
    for name, part, step in ((4, 0, 2), (5, 1, -2)):
        dkv_cps[name] = pltpu.make_async_remote_copy(
            src_ref=dkv_send.at[7, part], dst_ref=dkv_recv.at[7, part],
            send_sem=dkv_ss.at[name + 3], recv_sem=dkv_rs.at[name + 3],
            device_id=line_dev(step, c), device_id_type=MESH,
        )

    def queries_out(t):
        for i in range(4 * t, 4 * t + 4):
            if i > 0:
                dq_send[i] = dq_acc[i * ROWS : (i + 1) * ROWS, :].astype(BF16)
                dq_cps[i].start()

    def part(acc, i):
        return acc[i * ROWS : (i + 1) * ROWS, :]

    def to_sibling(dz):
        sib_send[dz + 3, 0] = part(dk_acc, THEIRS[dz]).astype(BF16)
        sib_send[dz + 3, 1] = part(dv_acc, THEIRS[dz]).astype(BF16)
        sib_cps[dz].start()

    def chip_sum(dz):
        sib_cps[dz].wait_recv()
        a = part(dk_acc, MINE[dz]) + sib_recv[dz + 3, 0].astype(F32)
        b = part(dv_acc, MINE[dz]) + sib_recv[dz + 3, 1].astype(F32)
        return a, b

    def to_owner(dz):
        a, b = chip_sum(dz)
        if dz in (1, -1):
            dkv_cps[3 * dz].wait_recv()
            a = a + dkv_recv[3 * dz + 3, 0].astype(F32)
            b = b + dkv_recv[3 * dz + 3, 1].astype(F32)
        if dz == 2:
            dkv_cps[4].wait_recv()
            a = a + dkv_recv[7, 0].astype(F32)
        if dz == -2:
            dkv_cps[5].wait_recv()
            b = b + dkv_recv[7, 1].astype(F32)
        dkv_send[dz + 3, 0] = a.astype(BF16)
        dkv_send[dz + 3, 1] = b.astype(BF16)
        dkv_cps[dz].start()
        if dz == 4:
            dkv_cps[5].start()

    def before(n):
        if n == 0:
            for offset in ((1, 0), (3, 0), (0, 1), (0, 3)):
                q_cps[at[offset]].wait_recv()
            for offset in ((1, 1), (3, 3), (1, 3), (3, 1)):
                q_cps[at[offset]].start()
            for dz in (1, -1):
                kz_cps[dz].wait_recv()
                kz_cps[3 * dz].start()
                kc_cps[dz].start()
            rows_of(0)
            kc_cps[0].wait_recv()
        if n == 1:
            for dz in (2, -2):
                kz_cps[dz].wait_recv()
                kz_cps[4 if dz == 2 else 5].start()
                kc_cps[dz].start()
            for offset in ((2, 0), (0, 2)):
                q_cps[at[offset]].wait_recv()
            for i in (at[1, 2], at[2, 1], at[3, 2], at[2, 3], far, 16):
                q_cps[i].start()
            kc_cps[1].wait_recv()
            kc_cps[-1].wait_recv()
        if n == 2:
            q_cps[at[1, 1]].wait_recv()
            rows_of(1)
        if n == 4:
            for dz in (3, -3):
                kz_cps[dz].wait_recv()
                kc_cps[dz].start()
            kc_cps[2].wait_recv()
            kc_cps[-2].wait_recv()
        if n == 5:
            kz_cps[4].wait_recv()
            kz_cps[5].wait_recv()
            kc_cps[4].start()
        if n == 6:
            for dz in (3, -3, 4):
                kc_cps[dz].wait_recv()
        if n == 8:
            queries_out(0)
            queries_out(1)
            for i in (8, 9, 10, 11, 16):
                q_cps[i].wait_recv()
            rows_of(2)
        if n == 9:
            for i in (12, 13, 14, 15):
                q_cps[i].wait_recv()
            rows_of(3)
        if n == 10:
            for dz in (4, 3, -3):
                to_sibling(dz)
        if n == 11:
            to_owner(4)
        if n == 12:
            to_owner(3)
            to_owner(-3)
            to_sibling(2)
            to_sibling(-2)
        if n == 14:
            queries_out(2)
        if n == 15:
            to_sibling(1)
            to_sibling(-1)
            to_owner(2)
            to_owner(-2)

    hooks = (0, 1, 2, 4, 5, 6, 8, 9, 10, 11, 12, 14, 15)

    def step(n, carry):
        for hook in hooks:
            pl.when(n == hook)(lambda hook=hook: before(hook))
        tile(pick([q for q, _ in TILES], n), pick([k for _, k in TILES], n))
        return carry

    lax.fori_loop(0, len(TILES), step, 0)

    to_sibling(0)
    to_owner(1)
    to_owner(-1)
    queries_out(3)

    a, b = chip_sum(0)
    total = dq_acc[0:ROWS, :]
    for i in range(1, 16):
        dq_cps[i].wait_recv()
        total = total + dq_recv[i].astype(F32)
    dq_out[...] = (total * SCALE).astype(BF16)
    for dz in (2, -2, 1, -1):
        dkv_cps[dz].wait_recv()
        a = a + dkv_recv[dz + 3, 0].astype(F32)
        b = b + dkv_recv[dz + 3, 1].astype(F32)
    dk_out[...] = (a * SCALE).astype(BF16)
    dv_out[...] = b.astype(BF16)

    for group in (q_cps, kz_cps, kc_cps, dq_cps, dkv_cps, sib_cps):
        for cp in group.values():
            cp.wait_send()


def per_device(queries, keys_in, values_in, outputs_saved, out_grad, log_sum, block_table):
    hbm = pl.BlockSpec(memory_space=pl.ANY)
    vmem = pl.BlockSpec(memory_space=pltpu.VMEM)
    smem = pl.BlockSpec(memory_space=pltpu.SMEM)
    dma = pltpu.SemaphoreType.DMA
    out = jax.ShapeDtypeStruct((ROWS, WIDTH), BF16)
    return pl.pallas_call(
        kernel,
        out_shape=(out, out, out),
        in_specs=[hbm, hbm, hbm, hbm, hbm, vmem, smem],
        out_specs=(vmem, vmem, vmem),
        scratch_shapes=[
            pltpu.VMEM((16, CHUNK, WIDTH), BF16),
            pltpu.VMEM((2, 16, ROWS, WIDTH), BF16),
            pltpu.VMEM((ROWS, WIDTH), BF16),
            pltpu.VMEM((16 * ROWS, WIDTH), F32),
            pltpu.VMEM((16 * ROWS, WIDTH), F32),
            pltpu.VMEM((16 * ROWS, WIDTH), F32),
            pltpu.VMEM((32, 16 * ROWS), F32),
            pltpu.VMEM((8, 16 * ROWS), F32),
            pltpu.VMEM((32, 128), jnp.int32),
            pltpu.VMEM((16, ROWS, WIDTH), BF16),
            pltpu.VMEM((16, ROWS, WIDTH), BF16),
            pltpu.VMEM((8, 2, ROWS, WIDTH), BF16),
            pltpu.VMEM((8, 2, ROWS, WIDTH), BF16),
            pltpu.VMEM((8, 2, ROWS, WIDTH), BF16),
            pltpu.VMEM((8, 2, ROWS, WIDTH), BF16),
            dma((5,)), dma((17,)), dma((17,)), dma((9,)), dma((9,)), dma((8,)), dma((8,)),
            dma((16,)), dma((16,)), dma((8,)), dma((8,)), dma((9,)), dma((9,)),
        ],
        compiler_params=pltpu.CompilerParams(
            collective_id=0, has_side_effects=True, vmem_limit_bytes=60 << 20
        ),
    )(
        queries, keys_in, values_in, outputs_saved, out_grad,
        log_sum.reshape(1, ROWS), block_table,
    )


def solution(mesh):
    rows = P(("pb", "ka"), None)
    return jax.shard_map(
        per_device,
        mesh=mesh,
        in_specs=(rows, rows, rows, rows, rows, P(("pb", "ka")), P()),
        out_specs=(rows, rows, rows),
        check_vma=False,
    )
```

time: 58.8 us -> 53.6 us (0.912)
  the two profiles are of different devices: /device:TPU:12 before, /device:TPU:2 now
where the time goes in v3:
time: 53.6 us; the launch traced here: 53.3 us
  Pallas kernels  49.9 us (93%)
  local copies, waits for them, and re-layouts  2.82 us (5%)
  between operations  0.65 us (1%)
    pallas_call x1, Pallas kernels, per_device(): pl.pallas_call(kernel, out_shape=(out, out, out), in_specs=[hbm, hbm, hbm...  49.9 us
    unnamed x7, local copies, waits for them, and re-layouts  2.82 us

profile of v3, /device:TPU:2, one launch (start us, length us, event | category | flops | bytes accessed | tf_op | source)
XLA Modules:
  0.0 53.3 jit_solution(10418630077641789236)
XLA Ops:
  0.6 49.9 %shard_map.94 = (bf16[160,128]{1,0:T(8,128)(2,1)}, bf16[160,128]{1,0:T(8,128)(2,1)}, bf16[160,128]{1,0:T(8,128)(2,1)}) custom-call(bf16[160,128]{1,0:T(8,128)(2,1)} %q_in.1, bf16[160,128]{1,0:T(8,128)(2,1)} %k_in.1, bf16[160,128]{1,0:T(8,128)(2,1)} %v_in.1, bf16[160,128]{1,0:T(8,128)(2,1)} %o_in.1, bf16[160,128]{1,0:T(8,128)(2,1)} %g_in.1, ...), custom_call_target="tpu_custom_call" | custom-call | tf_op jit(solution)/shard_map/pallas_call | solution.py:415
  50.5 0.0 copy-start.1
  50.5 1.4 %copy.13 = bf16[160,128]{1,0:T(8,128)(2,1)} copy(bf16[160,128]{1,0:T(8,128)(2,1)} %get-tuple-element.6) | data formatting | bytes 81920
  51.9 0.0 copy-done.1
  51.9 0.0 copy-start
  51.9 0.6 %copy.14 = bf16[160,128]{1,0:T(8,128)(2,1)} copy(bf16[160,128]{1,0:T(8,128)(2,1)S(1)} %copy-done.1) | data formatting | bytes 81920
  52.5 0.2 copy-done
  52.7 0.6 %copy.15 = bf16[160,128]{1,0:T(8,128)(2,1)} copy(bf16[160,128]{1,0:T(8,128)(2,1)S(1)} %copy-done) | data formatting | bytes 81920
Async XLA Ops:
  50.5 1.4 %copy-start.1 = (bf16[160,128]{1,0:T(8,128)(2,1)S(1)}, bf16[160,128]{1,0:T(8,128)(2,1)}, u32[]{:S(2)}) copy-start(bf16[160,128]{1,0:T(8,128)(2,1)} %get-tuple-element.7) | copy-start | bytes 122884
  51.9 0.8 %copy-start = (bf16[160,128]{1,0:T(8,128)(2,1)S(1)}, bf16[160,128]{1,0:T(8,128)(2,1)}, u32[]{:S(2)}) copy-start(bf16[160,128]{1,0:T(8,128)(2,1)} %get-tuple-element.8) | copy-start | bytes 122884

commit v4 on v3

--- a/solution.py
+++ b/solution.py
@@ -60,7 +60,7 @@
 
 def kernel(
     q_in, k_in, v_in, o_in, g_in, l_in, table,
-    dq_out, dk_out, dv_out,
+    out,
     qg, kv, o_own, dq_acc, dk_acc, dv_acc, lrow, drow, keyid,
     dq_send, dq_recv, sib_send, sib_recv, dkv_send, dkv_recv,
     local_sem, q_ss, q_rs, kz_ss, kz_rs, kc_ss, kc_rs,
@@ -84,20 +84,69 @@
         pl.semaphore_signal(barrier, inc=1, device_id=p, device_id_type=MESH)
 
     loads = [
-        pltpu.make_async_copy(g_in, qg.at[0, pl.ds(ROWS, ROWS)], local_sem.at[0]),
-        pltpu.make_async_copy(o_in, o_own, local_sem.at[1]),
-        pltpu.make_async_copy(q_in, qg.at[0, pl.ds(0, ROWS)], local_sem.at[2]),
-        pltpu.make_async_copy(k_in, kv.at[0, 0], local_sem.at[3]),
-        pltpu.make_async_copy(v_in, kv.at[1, 0], local_sem.at[4]),
+        pltpu.make_async_copy(k_in, kv.at[0, 0], local_sem.at[0]),
+        pltpu.make_async_copy(v_in, kv.at[1, 0], local_sem.at[1]),
+        pltpu.make_async_copy(g_in, qg.at[0, pl.ds(ROWS, ROWS)], local_sem.at[2]),
+        pltpu.make_async_copy(o_in, o_own, local_sem.at[3]),
+        pltpu.make_async_copy(q_in, qg.at[0, pl.ds(0, ROWS)], local_sem.at[4]),
     ]
     for cp in loads:
         cp.start()
-    dq_acc[...] = jnp.zeros_like(dq_acc)
-    dk_acc[...] = jnp.zeros_like(dk_acc)
-    dv_acc[...] = jnp.zeros_like(dv_acc)
-    for cp in loads:
+
+    def q_copy(i, held, dx, dy, sem, rows=(0, CHUNK)):
+        return pltpu.make_async_remote_copy(
+            src_ref=qg.at[held, pl.ds(*rows)], dst_ref=qg.at[i, pl.ds(*rows)],
+            send_sem=q_ss.at[sem], recv_sem=q_rs.at[sem],
+            device_id=device((x - dx + 4) % 4, (y - dy + 4) % 4, z, c), device_id_type=MESH,
+        )
+
+    at = {offset: i for i, offset in enumerate(PLANE)}
+    q_cps = {}
+    for offset in ((1, 0), (3, 0), (0, 1), (0, 3), (2, 0), (0, 2)):
+        q_cps[at[offset]] = q_copy(at[offset], 0, *offset, at[offset])
+    for dx, dy in ((1, 1), (3, 3), (1, 2), (3, 2)):
+        q_cps[at[dx, dy]] = q_copy(at[dx, dy], at[0, dy], dx, 0, at[dx, dy])
+    for dx, dy in ((1, 3), (3, 1), (2, 1), (2, 3)):
+        q_cps[at[dx, dy]] = q_copy(at[dx, dy], at[dx, 0], 0, dy, at[dx, dy])
+    far = at[2, 2]
+    q_cps[far] = q_copy(far, at[0, 2], 2, 0, far, (0, 176))
+    q_cps[16] = q_copy(far, at[2, 0], 0, 2, 16, (176, CHUNK - 176))
+
+    kz_cps = {}
+    for dz, (held, step) in {
+        1: (0, 1), -1: (0, -1), 2: (0, 2), -2: (0, -2), 3: (1, 2), -3: (-1, -2),
+    }.items():
+        kz_cps[dz] = pltpu.make_async_remote_copy(
+            src_ref=kv.at[:, MINE[held]], dst_ref=kv.at[:, MINE[dz]],
+            send_sem=kz_ss.at[dz + 3], recv_sem=kz_rs.at[dz + 3],
+            device_id=line_dev(-step, c), device_id_type=MESH,
+        )
+    for name, part, step in ((4, 0, 2), (5, 1, -2)):
+        kz_cps[name] = pltpu.make_async_remote_copy(
+            src_ref=kv.at[part, MINE[step]], dst_ref=kv.at[part, MINE[4]],
+            send_sem=kz_ss.at[name + 3], recv_sem=kz_rs.at[name + 3],
+            device_id=line_dev(-step, c), device_id_type=MESH,
+        )
+    kc_cps = {
+        dz: pltpu.make_async_remote_copy(
+            src_ref=kv.at[:, MINE[dz]], dst_ref=kv.at[:, THEIRS[dz]],
+            send_sem=kc_ss.at[dz + 3], recv_sem=kc_rs.at[dz + 3],
+            device_id=sibling, device_id_type=MESH,
+        )
+        for dz in MINE
+    }
+
+    for cp in loads[:2]:
         cp.wait()
-
+    pl.semaphore_wait(barrier, len(partners))
+    for dz in (1, -1):
+        kz_cps[dz].start()
+    kc_cps[0].start()
+    for dz in (2, -2):
+        kz_cps[dz].start()
+
+    for cp in loads[2:]:
+        cp.wait()
     q0, g0 = qg[0, 0:ROWS, :], qg[0, ROWS : 2 * ROWS, :]
     k0, v0 = kv[0, 0], kv[1, 0]
     prod = g0.astype(F32) * o_own[...].astype(F32)
@@ -126,55 +175,11 @@
     )
     qg[0, 2 * ROWS : CHUNK, :] = stats.astype(BF16)
 
-    def q_copy(i, held, dx, dy, sem, rows=(0, CHUNK)):
-        return pltpu.make_async_remote_copy(
-            src_ref=qg.at[held, pl.ds(*rows)], dst_ref=qg.at[i, pl.ds(*rows)],
-            send_sem=q_ss.at[sem], recv_sem=q_rs.at[sem],
-            device_id=device((x - dx + 4) % 4, (y - dy + 4) % 4, z, c), device_id_type=MESH,
-        )
-
-    at = {offset: i for i, offset in enumerate(PLANE)}
-    q_cps = {}
     for offset in ((1, 0), (3, 0), (0, 1), (0, 3), (2, 0), (0, 2)):
-        q_cps[at[offset]] = q_copy(at[offset], 0, *offset, at[offset])
-    for dx, dy in ((1, 1), (3, 3), (1, 2), (3, 2)):
-        q_cps[at[dx, dy]] = q_copy(at[dx, dy], at[0, dy], dx, 0, at[dx, dy])
-    for dx, dy in ((1, 3), (3, 1), (2, 1), (2, 3)):
-        q_cps[at[dx, dy]] = q_copy(at[dx, dy], at[dx, 0], 0, dy, at[dx, dy])
-    far = at[2, 2]
-    q_cps[far] = q_copy(far, at[0, 2], 2, 0, far, (0, 176))
-    q_cps[16] = q_copy(far, at[2, 0], 0, 2, 16, (176, CHUNK - 176))
-
-    kz_cps = {}
-    for dz, (held, step) in {
-        1: (0, 1), -1: (0, -1), 2: (0, 2), -2: (0, -2), 3: (1, 2), -3: (-1, -2),
-    }.items():
-        kz_cps[dz] = pltpu.make_async_remote_copy(
-            src_ref=kv.at[:, MINE[held]], dst_ref=kv.at[:, MINE[dz]],
-            send_sem=kz_ss.at[dz + 3], recv_sem=kz_rs.at[dz + 3],
-            device_id=line_dev(-step, c), device_id_type=MESH,
-        )
-    for name, part, step in ((4, 0, 2), (5, 1, -2)):
-        kz_cps[name] = pltpu.make_async_remote_copy(
-            src_ref=kv.at[part, MINE[step]], dst_ref=kv.at[part, MINE[4]],
-            send_sem=kz_ss.at[name + 3], recv_sem=kz_rs.at[name + 3],
-            device_id=line_dev(-step, c), device_id_type=MESH,
-        )
-    kc_cps = {
-        dz: pltpu.make_async_remote_copy(
-            src_ref=kv.at[:, MINE[dz]], dst_ref=kv.at[:, THEIRS[dz]],
-            send_sem=kc_ss.at[dz + 3], recv_sem=kc_rs.at[dz + 3],
-            device_id=sibling, device_id_type=MESH,
-        )
-        for dz in MINE
-    }
-
-    pl.semaphore_wait(barrier, len(partners))
-    for cp in (
-        kz_cps[1], kz_cps[-1], q_cps[at[1, 0]], q_cps[at[3, 0]], q_cps[at[0, 1]], q_cps[at[0, 3]],
-        kc_cps[0], kz_cps[2], kz_cps[-2], q_cps[at[2, 0]], q_cps[at[0, 2]],
-    ):
-        cp.start()
+        q_cps[at[offset]].start()
+    dq_acc[...] = jnp.zeros_like(dq_acc)
+    dk_acc[...] = jnp.zeros_like(dk_acc)
+    dv_acc[...] = jnp.zeros_like(dv_acc)
 
     row = lax.broadcasted_iota(jnp.int32, (ROWS, ROWS), 0)
     col = lax.broadcasted_iota(jnp.int32, (ROWS, ROWS), 1)
@@ -384,22 +389,22 @@
     lax.fori_loop(0, len(TILES), step, 0)
 
     to_sibling(0)
+    queries_out(3)
     to_owner(1)
     to_owner(-1)
-    queries_out(3)
 
     a, b = chip_sum(0)
     total = dq_acc[0:ROWS, :]
     for i in range(1, 16):
         dq_cps[i].wait_recv()
         total = total + dq_recv[i].astype(F32)
-    dq_out[...] = (total * SCALE).astype(BF16)
+    out[0] = (total * SCALE).astype(BF16)
     for dz in (2, -2, 1, -1):
         dkv_cps[dz].wait_recv()
         a = a + dkv_recv[dz + 3, 0].astype(F32)
         b = b + dkv_recv[dz + 3, 1].astype(F32)
-    dk_out[...] = (a * SCALE).astype(BF16)
-    dv_out[...] = b.astype(BF16)
+    out[1] = (a * SCALE).astype(BF16)
+    out[2] = b.astype(BF16)
 
     for group in (q_cps, kz_cps, kc_cps, dq_cps, dkv_cps, sib_cps):
         for cp in group.values():
@@ -411,12 +416,11 @@
     vmem = pl.BlockSpec(memory_space=pltpu.VMEM)
     smem = pl.BlockSpec(memory_space=pltpu.SMEM)
     dma = pltpu.SemaphoreType.DMA
-    out = jax.ShapeDtypeStruct((ROWS, WIDTH), BF16)
-    return pl.pallas_call(
+    sums = pl.pallas_call(
         kernel,
-        out_shape=(out, out, out),
+        out_shape=jax.ShapeDtypeStruct((3, ROWS, WIDTH), BF16),
         in_specs=[hbm, hbm, hbm, hbm, hbm, vmem, smem],
-        out_specs=(vmem, vmem, vmem),
+        out_specs=vmem,
         scratch_shapes=[
             pltpu.VMEM((16, CHUNK, WIDTH), BF16),
             pltpu.VMEM((2, 16, ROWS, WIDTH), BF16),
@@ -443,6 +447,7 @@
         queries, keys_in, values_in, outputs_saved, out_grad,
         log_sum.reshape(1, ROWS), block_table,
     )
+    return tuple(sums[i] for i in range(3))
 
 
 def solution(mesh):

time: 53.6 us -> 52 us (0.970)
  local copies, waits for them, and re-layouts: 2.82 us -> 1.47 us
    unnamed x7 -> x0, local copies, waits for them, and re-layouts: 2.82 us -> none
    squeeze x0 -> x1, local copies, waits for them, and re-layouts: none -> 1.47 us  [per_device(): return tuple((sums[i] for i in range(3)))]
where the time goes in v4:
time: 52 us; the launch traced here: 51.6 us
  Pallas kernels  49.4 us (95%)
  local copies, waits for them, and re-layouts  1.47 us (3%)
  between operations  0.64 us (1%)
    pallas_call x1, Pallas kernels, per_device(): pl.pallas_call(kernel, out_shape=jax.ShapeDtypeStruct((3, ROWS, WIDTH), B...  49.4 us
    squeeze x1, local copies, waits for them, and re-layouts, per_device(): return tuple((sums[i] for i in range(3)))  1.47 us

profile of v4, /device:TPU:2, one launch (start us, length us, event | category | flops | bytes accessed | tf_op | source)
XLA Modules:
  0.0 51.6 jit_solution(813833876480669924)
XLA Ops:
  0.6 49.4 %shard_map.94 = bf16[3,160,128]{2,1,0:T(8,128)(2,1)} custom-call(bf16[160,128]{1,0:T(8,128)(2,1)} %q_in.1, bf16[160,128]{1,0:T(8,128)(2,1)} %k_in.1, bf16[160,128]{1,0:T(8,128)(2,1)} %v_in.1, bf16[160,128]{1,0:T(8,128)(2,1)} %o_in.1, bf16[160,128]{1,0:T(8,128)(2,1)} %g_in.1, f32[1,160]{1,0:T(1,128)} %bitcast.7, s32[512]{0:T(512)} %table.1), custom_call_target="tpu_custom_call" | custom-call | tf_op jit(solution)/shard_map/pallas_call | solution.py:419
  50.1 1.5 %slice_bitcast_fusion = (bf16[160,128]{1,0:T(8,128)(2,1)}, bf16[160,128]{1,0:T(8,128)(2,1)}, bf16[160,128]{1,0:T(8,128)(2,1)}) fusion(bf16[3,160,128]{2,1,0:T(8,128)(2,1)} %shard_map.94), kind=kLoop, calls=%fused_computation | loop fusion | bytes 245760 | tf_op jit(solution)/shard_map/squeeze | solution.py:450

commit v5 on v4

--- a/solution.py
+++ b/solution.py
@@ -28,19 +28,12 @@
 MINE = {dz: LINE.index((dz, 0)) for dz in (0, 1, -1, 2, -2, 3, -3, 4)}
 THEIRS = {dz: LINE.index((dz, 1)) for dz in (0, 1, -1, 2, -2, 3, -3, 4)}
 TILES = (
-    (0, 0), (0, 1), (1, 1), (1, 0), (1, 2), (0, 2), (0, 3), (1, 3),
-    (2, 3), (3, 3), (3, 2), (2, 2), (2, 1), (2, 0), (3, 1), (3, 0),
+    (0, 0), (0, 1), (1, 1), (1, 0), (1, 2), (0, 2), (2, 2), (2, 3),
+    (3, 3), (0, 3), (1, 3), (3, 2), (2, 1), (2, 0), (3, 1), (3, 0),
 )
 Q_TILE, K_TILE = 4 * ROWS, 4 * ROWS
 NT = (((1,), (1,)), ((), ()))
 TN = (((0,), (0,)), ((), ()))
-
-
-def pick(values, n):
-    out = values[0]
-    for i in range(1, len(values)):
-        out = jnp.where(n == i, values[i], out)
-    return out
 
 
 def place():
@@ -77,7 +70,7 @@
         return device(x, y, (z + dz + 8) % 8, core)
 
     sibling = device(x, y, z, other)
-    partners = [plane_dev(i, 1) for i in range(1, 16)]
+    partners = [plane_dev(PLANE.index(at), 1) for at in ((1, 0), (3, 0), (0, 1), (0, 3), (2, 0), (0, 2))]
     partners += [line_dev(dz, c) for dz in (1, -1, 2, -2)] + [sibling]
     barrier = pltpu.get_barrier_semaphore()
     for p in partners:
@@ -226,15 +219,15 @@
                 )
 
     def tile(qi, ki):
-        qs = pl.ds(pl.multiple_of(qi * Q_TILE, Q_TILE), Q_TILE)
-        ks = pl.ds(pl.multiple_of(ki * K_TILE, K_TILE), K_TILE)
+        qs = pl.ds(qi * Q_TILE, Q_TILE)
+        ks = pl.ds(ki * K_TILE, K_TILE)
         q = qg[pl.ds(qi * 4, 4), 0:ROWS, :].reshape(Q_TILE, WIDTH)
         g = qg[pl.ds(qi * 4, 4), ROWS : 2 * ROWS, :].reshape(Q_TILE, WIDTH)
         k = kv[0, pl.ds(ki * 4, 4), :, :].reshape(K_TILE, WIDTH)
         v = kv[1, pl.ds(ki * 4, 4), :, :].reshape(K_TILE, WIDTH)
         s = lax.dot_general(k, q, NT, preferred_element_type=F32)
         dp = lax.dot_general(v, g, NT, preferred_element_type=F32)
-        lr = lrow[pl.ds(pl.multiple_of(ki * 8, 8), 8), qs]
+        lr = lrow[pl.ds(ki * 8, 8), qs]
         bias = jnp.broadcast_to(lr[:, None, :], (8, BLK, Q_TILE)).reshape(K_TILE, Q_TILE)
         p = jnp.exp2(s * TO_EXP2 - bias)
         ds = (p * (dp - drow[0:1, qs])).astype(BF16)
@@ -343,31 +336,28 @@
                 kc_cps[dz].start()
             kc_cps[2].wait_recv()
             kc_cps[-2].wait_recv()
-        if n == 5:
+        if n == 6:
             kz_cps[4].wait_recv()
             kz_cps[5].wait_recv()
             kc_cps[4].start()
-        if n == 6:
+            for i in (8, 9, 10, 11, 16):
+                q_cps[i].wait_recv()
+            rows_of(2)
+        if n == 7:
             for dz in (3, -3, 4):
                 kc_cps[dz].wait_recv()
         if n == 8:
-            queries_out(0)
-            queries_out(1)
-            for i in (8, 9, 10, 11, 16):
-                q_cps[i].wait_recv()
-            rows_of(2)
-        if n == 9:
             for i in (12, 13, 14, 15):
                 q_cps[i].wait_recv()
             rows_of(3)
-        if n == 10:
+        if n == 11:
             for dz in (4, 3, -3):
                 to_sibling(dz)
-        if n == 11:
-            to_owner(4)
+            queries_out(0)
+            queries_out(1)
         if n == 12:
-            to_owner(3)
-            to_owner(-3)
+            for dz in (4, 3, -3):
+                to_owner(dz)
             to_sibling(2)
             to_sibling(-2)
         if n == 14:
@@ -375,23 +365,16 @@
         if n == 15:
             to_sibling(1)
             to_sibling(-1)
-            to_owner(2)
-            to_owner(-2)
-
-    hooks = (0, 1, 2, 4, 5, 6, 8, 9, 10, 11, 12, 14, 15)
-
-    def step(n, carry):
-        for hook in hooks:
-            pl.when(n == hook)(lambda hook=hook: before(hook))
-        tile(pick([q for q, _ in TILES], n), pick([k for _, k in TILES], n))
-        return carry
-
-    lax.fori_loop(0, len(TILES), step, 0)
+
+
+    for n, (qi, ki) in enumerate(TILES):
+        before(n)
+        tile(qi, ki)
 
     to_sibling(0)
     queries_out(3)
-    to_owner(1)
-    to_owner(-1)
+    for dz in (2, -2, 1, -1):
+        to_owner(dz)
 
     a, b = chip_sum(0)
     total = dq_acc[0:ROWS, :]

time: 52 us -> 50.6 us (0.973)
  Pallas kernels: 49.4 us -> 48.1 us
    pallas_call x1, Pallas kernels: 49.4 us -> 48.1 us  [per_device(): pl.pallas_call(kernel, out_shape=jax.ShapeDtypeStruct((3, ROWS, WIDTH), B...]
where the time goes in v5:
time: 50.6 us; the launch traced here: 50.2 us
  Pallas kernels  48.1 us (95%)
  local copies, waits for them, and re-layouts  1.47 us (3%)
  between operations  0.64 us (1%)
    pallas_call x1, Pallas kernels, per_device(): pl.pallas_call(kernel, out_shape=jax.ShapeDtypeStruct((3, ROWS, WIDTH), B...  48.1 us
    squeeze x1, local copies, waits for them, and re-layouts, per_device(): return tuple((sums[i] for i in range(3)))  1.47 us

profile of v5, /device:TPU:2, one launch (start us, length us, event | category | flops | bytes accessed | tf_op | source)
XLA Modules:
  0.0 50.2 jit_solution(9948703763696838296)
XLA Ops:
  0.6 48.1 %shard_map.94 = bf16[3,160,128]{2,1,0:T(8,128)(2,1)} custom-call(bf16[160,128]{1,0:T(8,128)(2,1)} %q_in.1, bf16[160,128]{1,0:T(8,128)(2,1)} %k_in.1, bf16[160,128]{1,0:T(8,128)(2,1)} %v_in.1, bf16[160,128]{1,0:T(8,128)(2,1)} %o_in.1, bf16[160,128]{1,0:T(8,128)(2,1)} %g_in.1, f32[1,160]{1,0:T(1,128)} %bitcast.7, s32[512]{0:T(512)} %table.1), custom_call_target="tpu_custom_call" | custom-call | tf_op jit(solution)/shard_map/pallas_call | solution.py:402
  48.7 1.5 %slice_bitcast_fusion = (bf16[160,128]{1,0:T(8,128)(2,1)}, bf16[160,128]{1,0:T(8,128)(2,1)}, bf16[160,128]{1,0:T(8,128)(2,1)}) fusion(bf16[3,160,128]{2,1,0:T(8,128)(2,1)} %shard_map.94), kind=kLoop, calls=%fused_computation | loop fusion | bytes 245760 | tf_op jit(solution)/shard_map/squeeze | solution.py:433

commit v6 on v5

--- a/solution.py
+++ b/solution.py
@@ -52,9 +52,9 @@
 
 
 def kernel(
-    q_in, k_in, v_in, o_in, g_in, l_in, table,
+    q_in, k_in, v_in, o_in, g_in, l_in, table_in,
     out,
-    qg, kv, o_own, dq_acc, dk_acc, dv_acc, lrow, drow, keyid,
+    qg, kv, o_own, l_own, table, dq_acc, dk_acc, dv_acc, lrow, drow, keyid,
     dq_send, dq_recv, sib_send, sib_recv, dkv_send, dkv_recv,
     local_sem, q_ss, q_rs, kz_ss, kz_rs, kc_ss, kc_rs,
     dq_ss, dq_rs, sib_ss, sib_rs, dkv_ss, dkv_rs,
@@ -82,6 +82,8 @@
         pltpu.make_async_copy(g_in, qg.at[0, pl.ds(ROWS, ROWS)], local_sem.at[2]),
         pltpu.make_async_copy(o_in, o_own, local_sem.at[3]),
         pltpu.make_async_copy(q_in, qg.at[0, pl.ds(0, ROWS)], local_sem.at[4]),
+        pltpu.make_async_copy(l_in, l_own, local_sem.at[5]),
+        pltpu.make_async_copy(table_in, table, local_sem.at[6]),
     ]
     for cp in loads:
         cp.start()
@@ -149,7 +151,7 @@
     delta8 = lax.dot_general(ones, high, NT, preferred_element_type=F32)
     delta8 += lax.dot_general(ones, low, NT, preferred_element_type=F32)
     delta = delta8[0:1, :]
-    lse = l_in[...] * LOG2E
+    lse = l_own[...] * LOG2E
     sub = lax.broadcasted_iota(jnp.int32, (8, ROWS), 0)
     both = jnp.where(sub % 2 == 0, lse, delta)
     p1 = both.astype(BF16).astype(F32)
@@ -397,17 +399,18 @@
 def per_device(queries, keys_in, values_in, outputs_saved, out_grad, log_sum, block_table):
     hbm = pl.BlockSpec(memory_space=pl.ANY)
     vmem = pl.BlockSpec(memory_space=pltpu.VMEM)
-    smem = pl.BlockSpec(memory_space=pltpu.SMEM)
     dma = pltpu.SemaphoreType.DMA
     sums = pl.pallas_call(
         kernel,
         out_shape=jax.ShapeDtypeStruct((3, ROWS, WIDTH), BF16),
-        in_specs=[hbm, hbm, hbm, hbm, hbm, vmem, smem],
+        in_specs=[hbm] * 7,
         out_specs=vmem,
         scratch_shapes=[
             pltpu.VMEM((16, CHUNK, WIDTH), BF16),
             pltpu.VMEM((2, 16, ROWS, WIDTH), BF16),
             pltpu.VMEM((ROWS, WIDTH), BF16),
+            pltpu.VMEM((1, ROWS), F32),
+            pltpu.SMEM((512,), jnp.int32),
             pltpu.VMEM((16 * ROWS, WIDTH), F32),
             pltpu.VMEM((16 * ROWS, WIDTH), F32),
             pltpu.VMEM((16 * ROWS, WIDTH), F32),
@@ -420,7 +423,7 @@
             pltpu.VMEM((8, 2, ROWS, WIDTH), BF16),
             pltpu.VMEM((8, 2, ROWS, WIDTH), BF16),
             pltpu.VMEM((8, 2, ROWS, WIDTH), BF16),
-            dma((5,)), dma((17,)), dma((17,)), dma((9,)), dma((9,)), dma((8,)), dma((8,)),
+            dma((7,)), dma((17,)), dma((17,)), dma((9,)), dma((9,)), dma((8,)), dma((8,)),
             dma((16,)), dma((16,)), dma((8,)), dma((8,)), dma((9,)), dma((9,)),
         ],
         compiler_params=pltpu.CompilerParams(

time: 50.6 us -> 49.8 us (0.984)
  Pallas kernels: 48.1 us -> 47.3 us
    pallas_call x1, Pallas kernels: 48.1 us -> 47.3 us  [per_device(): pl.pallas_call(kernel, out_shape=jax.ShapeDtypeStruct((3, ROWS, WIDTH), B...]
where the time goes in v6:
time: 49.8 us; the launch traced here: 49.4 us
  Pallas kernels  47.3 us (95%)
  local copies, waits for them, and re-layouts  1.47 us (3%)
  between operations  0.64 us (1%)
    pallas_call x1, Pallas kernels, per_device(): pl.pallas_call(kernel, out_shape=jax.ShapeDtypeStruct((3, ROWS, WIDTH), B...  47.3 us
    squeeze x1, local copies, waits for them, and re-layouts, per_device(): return tuple((sums[i] for i in range(3)))  1.47 us

profile of v6, /device:TPU:2, one launch (start us, length us, event | category | flops | bytes accessed | tf_op | source)
XLA Modules:
  0.0 49.4 jit_solution(9961481796163113253)
XLA Ops:
  0.6 47.3 %shard_map.94 = bf16[3,160,128]{2,1,0:T(8,128)(2,1)} custom-call(bf16[160,128]{1,0:T(8,128)(2,1)} %q_in.1, bf16[160,128]{1,0:T(8,128)(2,1)} %k_in.1, bf16[160,128]{1,0:T(8,128)(2,1)} %v_in.1, bf16[160,128]{1,0:T(8,128)(2,1)} %o_in.1, bf16[160,128]{1,0:T(8,128)(2,1)} %g_in.1, f32[1,160]{1,0:T(1,128)} %bitcast.7, s32[512]{0:T(512)} %table_in.1), custom_call_target="tpu_custom_call" | custom-call | tf_op jit(solution)/shard_map/pallas_call | solution.py:403
  47.9 1.5 %slice_bitcast_fusion = (bf16[160,128]{1,0:T(8,128)(2,1)}, bf16[160,128]{1,0:T(8,128)(2,1)}, bf16[160,128]{1,0:T(8,128)(2,1)}) fusion(bf16[3,160,128]{2,1,0:T(8,128)(2,1)} %shard_map.94), kind=kLoop, calls=%fused_computation | loop fusion | bytes 245760 | tf_op jit(solution)/shard_map/squeeze | solution.py:436

commit v7 on v6

--- a/solution.py
+++ b/solution.py
@@ -28,8 +28,8 @@
 MINE = {dz: LINE.index((dz, 0)) for dz in (0, 1, -1, 2, -2, 3, -3, 4)}
 THEIRS = {dz: LINE.index((dz, 1)) for dz in (0, 1, -1, 2, -2, 3, -3, 4)}
 TILES = (
-    (0, 0), (0, 1), (1, 1), (1, 0), (1, 2), (0, 2), (2, 2), (2, 3),
-    (3, 3), (0, 3), (1, 3), (3, 2), (2, 1), (2, 0), (3, 1), (3, 0),
+    (0, 0, 1), (0, 1, 1), (1, 1, 1), (1, 0, 1), (0, 2, 2), (2, 2, 1), (2, 3, 2),
+    (0, 3, 2), (3, 2, 1), (2, 1, 1), (2, 0, 1), (3, 1, 1), (3, 0, 1),
 )
 Q_TILE, K_TILE = 4 * ROWS, 4 * ROWS
 NT = (((1,), (1,)), ((), ()))
@@ -220,17 +220,18 @@
                     ids > keyid[8 * u : 8 * u + 8, :], lb, HIDDEN
                 )
 
-    def tile(qi, ki):
-        qs = pl.ds(qi * Q_TILE, Q_TILE)
+    def tile(qi, ki, wide):
+        n_queries = wide * Q_TILE
+        qs = pl.ds(qi * Q_TILE, n_queries)
         ks = pl.ds(ki * K_TILE, K_TILE)
-        q = qg[pl.ds(qi * 4, 4), 0:ROWS, :].reshape(Q_TILE, WIDTH)
-        g = qg[pl.ds(qi * 4, 4), ROWS : 2 * ROWS, :].reshape(Q_TILE, WIDTH)
+        q = qg[pl.ds(qi * 4, wide * 4), 0:ROWS, :].reshape(n_queries, WIDTH)
+        g = qg[pl.ds(qi * 4, wide * 4), ROWS : 2 * ROWS, :].reshape(n_queries, WIDTH)
         k = kv[0, pl.ds(ki * 4, 4), :, :].reshape(K_TILE, WIDTH)
         v = kv[1, pl.ds(ki * 4, 4), :, :].reshape(K_TILE, WIDTH)
         s = lax.dot_general(k, q, NT, preferred_element_type=F32)
         dp = lax.dot_general(v, g, NT, preferred_element_type=F32)
         lr = lrow[pl.ds(ki * 8, 8), qs]
-        bias = jnp.broadcast_to(lr[:, None, :], (8, BLK, Q_TILE)).reshape(K_TILE, Q_TILE)
+        bias = jnp.broadcast_to(lr[:, None, :], (8, BLK, n_queries)).reshape(K_TILE, n_queries)
         p = jnp.exp2(s * TO_EXP2 - bias)
         ds = (p * (dp - drow[0:1, qs])).astype(BF16)
         dv_acc[ks, :] += jnp.dot(p.astype(BF16), g, preferred_element_type=F32)
@@ -338,40 +339,38 @@
                 kc_cps[dz].start()
             kc_cps[2].wait_recv()
             kc_cps[-2].wait_recv()
-        if n == 6:
+        if n == 5:
             kz_cps[4].wait_recv()
             kz_cps[5].wait_recv()
             kc_cps[4].start()
             for i in (8, 9, 10, 11, 16):
                 q_cps[i].wait_recv()
             rows_of(2)
-        if n == 7:
+        if n == 6:
+            for i in (12, 13, 14, 15):
+                q_cps[i].wait_recv()
+            rows_of(3)
             for dz in (3, -3, 4):
                 kc_cps[dz].wait_recv()
         if n == 8:
-            for i in (12, 13, 14, 15):
-                q_cps[i].wait_recv()
-            rows_of(3)
-        if n == 11:
             for dz in (4, 3, -3):
                 to_sibling(dz)
             queries_out(0)
             queries_out(1)
-        if n == 12:
+        if n == 9:
             for dz in (4, 3, -3):
                 to_owner(dz)
             to_sibling(2)
             to_sibling(-2)
-        if n == 14:
+        if n == 11:
             queries_out(2)
-        if n == 15:
+        if n == 12:
             to_sibling(1)
             to_sibling(-1)
 
-
-    for n, (qi, ki) in enumerate(TILES):
+    for n, (qi, ki, wide) in enumerate(TILES):
         before(n)
-        tile(qi, ki)
+        tile(qi, ki, wide)
 
     to_sibling(0)
     queries_out(3)

time: 49.8 us -> 49.7 us (level)
  no operation moved by 1% of the time
where the time goes in v7:
time: 49.7 us; the launch traced here: 49.3 us
  Pallas kernels  47.2 us (95%)
  local copies, waits for them, and re-layouts  1.47 us (3%)
  between operations  0.64 us (1%)
    pallas_call x1, Pallas kernels, per_device(): pl.pallas_call(kernel, out_shape=jax.ShapeDtypeStruct((3, ROWS, WIDTH), B...  47.2 us
    squeeze x1, local copies, waits for them, and re-layouts, per_device(): return tuple((sums[i] for i in range(3)))  1.47 us

profile of v7, /device:TPU:2, one launch (start us, length us, event | category | flops | bytes accessed | tf_op | source)
XLA Modules:
  0.0 49.3 jit_solution(2818955028673854385)
XLA Ops:
  0.6 47.2 %shard_map.94 = bf16[3,160,128]{2,1,0:T(8,128)(2,1)} custom-call(bf16[160,128]{1,0:T(8,128)(2,1)} %q_in.1, bf16[160,128]{1,0:T(8,128)(2,1)} %k_in.1, bf16[160,128]{1,0:T(8,128)(2,1)} %v_in.1, bf16[160,128]{1,0:T(8,128)(2,1)} %o_in.1, bf16[160,128]{1,0:T(8,128)(2,1)} %g_in.1, f32[1,160]{1,0:T(1,128)} %bitcast.7, s32[512]{0:T(512)} %table_in.1), custom_call_target="tpu_custom_call" | custom-call | tf_op jit(solution)/shard_map/pallas_call | solution.py:402
  47.8 1.5 %slice_bitcast_fusion = (bf16[160,128]{1,0:T(8,128)(2,1)}, bf16[160,128]{1,0:T(8,128)(2,1)}, bf16[160,128]{1,0:T(8,128)(2,1)}) fusion(bf16[3,160,128]{2,1,0:T(8,128)(2,1)} %shard_map.94), kind=kLoop, calls=%fused_computation | loop fusion | bytes 245760 | tf_op jit(solution)/shard_map/squeeze | solution.py:435

commit v8 on v7

--- a/solution.py
+++ b/solution.py
@@ -53,8 +53,8 @@
 
 def kernel(
     q_in, k_in, v_in, o_in, g_in, l_in, table_in,
-    out,
-    qg, kv, o_own, l_own, table, dq_acc, dk_acc, dv_acc, lrow, drow, keyid,
+    out_hbm,
+    out, qg, kv, o_own, l_own, table, dq_acc, dk_acc, dv_acc, lrow, drow, keyid,
     dq_send, dq_recv, sib_send, sib_recv, dkv_send, dkv_recv,
     local_sem, q_ss, q_rs, kz_ss, kz_rs, kc_ss, kc_rs,
     dq_ss, dq_rs, sib_ss, sib_rs, dkv_ss, dkv_rs,
@@ -383,28 +383,34 @@
         dq_cps[i].wait_recv()
         total = total + dq_recv[i].astype(F32)
     out[0] = (total * SCALE).astype(BF16)
+    first_out = pltpu.make_async_copy(out.at[0], out_hbm.at[0], local_sem.at[7])
+    first_out.start()
     for dz in (2, -2, 1, -1):
         dkv_cps[dz].wait_recv()
         a = a + dkv_recv[dz + 3, 0].astype(F32)
         b = b + dkv_recv[dz + 3, 1].astype(F32)
     out[1] = (a * SCALE).astype(BF16)
     out[2] = b.astype(BF16)
+    rest_out = pltpu.make_async_copy(out.at[pl.ds(1, 2)], out_hbm.at[pl.ds(1, 2)], local_sem.at[8])
+    rest_out.start()
 
     for group in (q_cps, kz_cps, kc_cps, dq_cps, dkv_cps, sib_cps):
         for cp in group.values():
             cp.wait_send()
+    first_out.wait()
+    rest_out.wait()
 
 
 def per_device(queries, keys_in, values_in, outputs_saved, out_grad, log_sum, block_table):
     hbm = pl.BlockSpec(memory_space=pl.ANY)
-    vmem = pl.BlockSpec(memory_space=pltpu.VMEM)
     dma = pltpu.SemaphoreType.DMA
     sums = pl.pallas_call(
         kernel,
         out_shape=jax.ShapeDtypeStruct((3, ROWS, WIDTH), BF16),
         in_specs=[hbm] * 7,
-        out_specs=vmem,
+        out_specs=hbm,
         scratch_shapes=[
+            pltpu.VMEM((3, ROWS, WIDTH), BF16),
             pltpu.VMEM((16, CHUNK, WIDTH), BF16),
             pltpu.VMEM((2, 16, ROWS, WIDTH), BF16),
             pltpu.VMEM((ROWS, WIDTH), BF16),
@@ -422,7 +428,7 @@
             pltpu.VMEM((8, 2, ROWS, WIDTH), BF16),
             pltpu.VMEM((8, 2, ROWS, WIDTH), BF16),
             pltpu.VMEM((8, 2, ROWS, WIDTH), BF16),
-            dma((7,)), dma((17,)), dma((17,)), dma((9,)), dma((9,)), dma((8,)), dma((8,)),
+            dma((9,)), dma((17,)), dma((17,)), dma((9,)), dma((9,)), dma((8,)), dma((8,)),
             dma((16,)), dma((16,)), dma((8,)), dma((8,)), dma((9,)), dma((9,)),
         ],
         compiler_params=pltpu.CompilerParams(

time: 49.7 us -> 49.6 us (level)
  no operation moved by 1% of the time
where the time goes in v8:
time: 49.6 us; the launch traced here: 49.2 us
  Pallas kernels  47.1 us (95%)
  local copies, waits for them, and re-layouts  1.47 us (3%)
  between operations  0.64 us (1%)
    pallas_call x1, Pallas kernels, per_device(): pl.pallas_call(kernel, out_shape=jax.ShapeDtypeStruct((3, ROWS, WIDTH), B...  47.1 us
    squeeze x1, local copies, waits for them, and re-layouts, per_device(): return tuple((sums[i] for i in range(3)))  1.47 us

profile of v8, /device:TPU:2, one launch (start us, length us, event | category | flops | bytes accessed | tf_op | source)
XLA Modules:
  0.0 49.2 jit_solution(16137514191606915357)
XLA Ops:
  0.6 47.1 %shard_map.94 = bf16[3,160,128]{2,1,0:T(8,128)(2,1)} custom-call(bf16[160,128]{1,0:T(8,128)(2,1)} %q_in.1, bf16[160,128]{1,0:T(8,128)(2,1)} %k_in.1, bf16[160,128]{1,0:T(8,128)(2,1)} %v_in.1, bf16[160,128]{1,0:T(8,128)(2,1)} %o_in.1, bf16[160,128]{1,0:T(8,128)(2,1)} %g_in.1, f32[1,160]{1,0:T(1,128)} %bitcast.7, s32[512]{0:T(512)} %table_in.1), custom_call_target="tpu_custom_call" | custom-call | tf_op jit(solution)/shard_map/pallas_call | solution.py:407
  47.7 1.5 %slice_bitcast_fusion = (bf16[160,128]{1,0:T(8,128)(2,1)}, bf16[160,128]{1,0:T(8,128)(2,1)}, bf16[160,128]{1,0:T(8,128)(2,1)}) fusion(bf16[3,160,128]{2,1,0:T(8,128)(2,1)} %shard_map.94), kind=kLoop, calls=%fused_computation | loop fusion | bytes 245760 | tf_op jit(solution)/shard_map/squeeze | solution.py:441
